TPU v7x, 32 devices: a whole 2x2x4 slice. The times are simulated.
32 devices in a mesh: groups: 2 (over y), tensor: 4 (over z), section: 4 (over x, core).
Axes of the slice: x: 2, y: 2, z: 4, core: 2. Of those that a mesh axis runs over, the one named last changes fastest.
Arguments:
- prefill_x: bfloat16 [4096, 8192], P(('groups', 'section'), 'tensor'), parts along dimension 0, may hold values from -6 to 6
- norm_gain: float32 [8192], replicated, may hold values from 0.5 to 2
- w_q: bfloat16 [8192, 8192], P(None, 'tensor'), may hold values from -127 to 127, as said below
- q_scale: float32 [8192], P('tensor'), may hold values from 7.7339806e-05 to 0.00030935922
- key_value_weight: bfloat16 [8192, 2048], P(None, 'tensor'), may hold values from -127 to 127, as said below
- key_value_scale: float32 [2048], P('tensor'), may hold values from 7.7339806e-05 to 0.00030935922
- w_o: bfloat16 [8192, 8192], P('tensor'), may hold values from -127 to 127, as said below
- o_scale: float32 [8192], P('tensor'), may hold values from 0.0022097088 to 0.008838835
- prefix_cache: bfloat16 [4, 32, 2048, 512], P('tensor', ('groups', 'section')), parts along dimension 1, may hold values from -2048 to 2048, as said below
- prefix_len: int32 [32], P(('groups', 'section')), parts along dimension 0, may hold values from 512 to 2048, as said below
- dec_x: bfloat16 [2, 256, 8192], P(None, ('groups', 'section'), 'tensor'), parts along dimension 1, may hold values from -6 to 6
- dec_cache: bfloat16 [4, 256, 64, 512], P('tensor', ('groups', 'section')), parts along dimension 1, may hold values from -2048 to 2048, as said below
- dec_len: int32 [256], P(('groups', 'section')), parts along dimension 0, may hold values from 16 to 64, as said below
- place: int32 [32], P('groups'), parts along dimension 0, may hold values from 0 to 127, as said below
Outputs:
- prefill_out: bfloat16 [4096, 8192], P(('groups', 'section'), 'tensor'), parts along dimension 0
- decode_out: bfloat16 [2, 256, 8192], P(None, ('groups', 'section'), 'tensor'), parts along dimension 1
There are 2 independent parts, one for each index of `groups`. A program takes and returns all parts, laid end to end along the dimension named above; an argument that names none is the same for every part. Nothing has to cross between parts.
Inputs may be any that keep to these rules, and one draw needn't show every extreme that they name: `w_q`: integers, int8 weight values. `key_value_weight`: integers, int8 weight values. `w_o`: integers, int8 weight values. `prefix_cache`: copies of one kv head on different tensor indices are equal. `dec_cache`: copies of one kv head on different tensor indices are equal. `prefix_len`: some prompt has exactly 2048 live positions. `dec_len`: some decode row has exactly 64 live positions. place[s * 4 + p] = o * 32 + r sends prompt p of section index s to decode row r of owner section index o; no two prompts share a decode row; one section index sends at most 2 prompts to one owner, and in every draw some owner receives 2 prompts from every section index.
All inputs are finite; a program needn't handle non-finite values.
Results may differ from a plain program's by a relative error of at most 0.024.
Values may be sent and summed in bfloat16 or wider, within the bound.
No kernel may reach another device: no remote copies, remote signals or barrier semaphores. Data moves between devices by JAX's collectives and lax.ppermute only.
A program may use at most 192 MiB of HBM per device.

v0:
```python
import functools
import math

import jax
import jax.numpy as jnp
from jax import lax
from jax.experimental import pallas as pl
from jax.experimental.pallas import tpu as pltpu
from jax.sharding import PartitionSpec as P

HEAD_SIZE = 128
PROMPT_TOKENS = 128
KERNEL_VMEM = 36 << 20
WEIGHT_BUFFERS = 8
COST_SHARE = 256
EXP2_FACTOR = math.log2(math.e) / math.sqrt(HEAD_SIZE)
MASKED = -1e30


def partner_2(block, axis, distance):
    count = lax.axis_size(axis)
    route = []
    for low in range(count):
        high = low | 1 << distance
        if high != low and high < count:
            route += [(low, high), (high, low)]
    return lax.ppermute(block, axis, route)


def joined(portion, partner, bit_number, concat_dim, tensor_index):
    upper_half = tensor_index // 2**bit_number % 2 == 1
    lower_first = jnp.concatenate([portion, partner], axis=concat_dim)
    upper_first = jnp.concatenate([partner, portion], axis=concat_dim)
    return jnp.where(upper_half, upper_first, lower_first)


def tile_of(extent, most):
    tile = extent
    while tile > most and tile % 2 == 0:
        tile //= 2
    return tile


def after(value, *others):
    return lax.optimization_barrier((value,) + others)[0]


def after_all(values, *others):
    return lax.optimization_barrier(tuple(values) + others)[: len(values)]


def line_order(index):
    low = index < 2
    return [index, index ^ 1, jnp.where(low, 2, 1), jnp.where(low, 3, 0)]


OUTER = [(0, 1), (1, 0), (2, 3), (3, 2)]
MIDDLE = [(1, 2), (2, 1)]
INWARD = [(0, 1), (3, 2)]
OUTWARD = [(1, 0), (2, 3)]


class LineGather:
    def __init__(self, block, axis, outer_held=(), middle_held=()):
        self.block, self.axis = block, axis
        self.partner = lax.ppermute(after(block, *outer_held), axis, OUTER)
        self.middle = lax.ppermute(after(block, *middle_held), axis, MIDDLE)

    def second(self, *held):
        partner, middle = after_all((self.partner, self.middle), *held)
        self.outer = lax.ppermute(middle, self.axis, OUTWARD)
        self.middle_far = lax.ppermute(partner, self.axis, MIDDLE)

    def third(self, *held):
        self.outer_far = lax.ppermute(after(self.middle_far, *held), self.axis, OUTWARD)

    def slots(self):
        return [
            [self.block],
            [self.partner],
            [self.middle, self.outer],
            [self.middle_far, self.outer_far],
        ]


def corners(arrays):
    return [array[:HEAD_SIZE, :HEAD_SIZE] for array in arrays]


def added(*terms):
    total = sum(term.astype(jnp.float32) for term in terms)
    return total.astype(terms[0].dtype)


class LineScatter:
    def __init__(self, own, partner, near, far, axis):
        self.own, self.partner, self.near, self.far = own, partner, near, far
        self.axis = axis
        self.far_in = lax.ppermute(far, axis, INWARD)

    def second(self, *held):
        far, near = after_all((added(self.far, self.far_in), self.near), *held)
        self.first_hop = (far,)
        self.near_in = lax.ppermute(near, self.axis, INWARD)
        self.far_out = lax.ppermute(far, self.axis, MIDDLE)

    def third(self, *held):
        self.third_begin()
        self.third_start(*held)

    def third_begin(self):
        self.second_hop = (
            added(self.near, self.near_in),
            added(self.partner, self.far_out),
        )

    def third_start(self, *held):
        near, partner = after_all(self.second_hop, *held)
        near = lax.ppermute(near, self.axis, MIDDLE)
        partner = lax.ppermute(partner, self.axis, OUTER)
        self.terms = [self.own, near, partner]


def in_hbm(arrays):
    return [pltpu.with_memory_space_constraint(array, pltpu.HBM) for array in arrays]


def without(kernel, first, count):
    return lambda *refs: kernel(*refs[:first], *refs[first + count :])


def qkv_kernel(counts, begun, ended, tile, order, *refs):
    refs = list(refs)
    arrays = sum(counts)
    xs = [refs.pop(0) for _ in range(arrays)]
    gain_ref, wq_ref, wkv_ref = (refs.pop(0) for _ in range(3))
    sums_in = [refs.pop(0) for _ in range(3)] if begun else []
    if ended:
        qs_ref, kvs_ref, q_ref, kv_ref, accq, acckv, squares = (refs.pop(0) for _ in range(7))
    else:
        accq, acckv, squares = (refs.pop(0) for _ in range(3))
    x_bufs = [refs.pop(0) for _ in range(arrays)]
    wq_buf, wkv_buf, x_sem, w_sem, sum_sem = refs
    per = x_bufs[0].shape[1] // tile
    steps = len(counts) * per
    ahead = min(steps, wq_buf.shape[0])

    def weight_copies(step):
        buffer = lax.rem(step, ahead)
        at = pl.multiple_of((order[step // per] * per + lax.rem(step, per)) * tile, tile)
        return [
            pltpu.make_async_copy(ref.at[pl.ds(at, tile)], buf.at[buffer], w_sem.at[w, buffer])
            for w, (ref, buf) in enumerate([(wq_ref, wq_buf), (wkv_ref, wkv_buf)])
        ]

    x_copies = [
        pltpu.make_async_copy(ref, buf, x_sem.at[a]) for a, (ref, buf) in enumerate(zip(xs, x_bufs))
    ]
    sum_copies = [
        pltpu.make_async_copy(ref, acc, sum_sem.at[a])
        for a, (ref, acc) in enumerate(zip(sums_in, (accq, acckv, squares)))
    ]
    for copy in x_copies[: counts[0]] + sum_copies:
        copy.start()
    for step in range(ahead):
        for copy in weight_copies(step):
            copy.start()
    for copy in x_copies[counts[0] :]:
        copy.start()
    for copy in sum_copies:
        copy.wait()
    if not begun:
        accq[...] = jnp.zeros_like(accq)
        acckv[...] = jnp.zeros_like(acckv)
        squares[...] = jnp.zeros_like(squares)

    taken = 0
    for s, count in enumerate(counts):
        for copy in x_copies[taken : taken + count]:
            copy.wait()
        bufs = x_bufs[taken : taken + count]
        taken += count

        def body(j, carry, s=s, bufs=bufs):
            step = s * per + j
            for copy in weight_copies(step):
                copy.wait()
            at = pl.multiple_of(j * tile, tile)
            values = sum(buf[:, pl.ds(at, tile)].astype(jnp.float32) for buf in bufs)
            gain = gain_ref[:, pl.ds(pl.multiple_of((order[s] * per + j) * tile, tile), tile)]
            squares[...] += jnp.broadcast_to(
                jnp.sum(values * values, axis=-1, keepdims=True), squares.shape
            )
            scaled = (values * gain).astype(jnp.bfloat16)
            buffer = lax.rem(step, ahead)
            accq[...] += jnp.dot(scaled, wq_buf[buffer], preferred_element_type=jnp.float32)
            acckv[...] += jnp.dot(scaled, wkv_buf[buffer], preferred_element_type=jnp.float32)

            @pl.when(step + ahead < steps)
            def _():
                for copy in weight_copies(step + ahead):
                    copy.start()

            return carry

        lax.fori_loop(0, per, body, 0)
    if ended:
        root = lax.rsqrt(squares[:, :1] / ended + 1e-05)
        q_ref[...] = (accq[...] * root * qs_ref[...]).astype(q_ref.dtype)
        kv_ref[...] = (acckv[...] * root * kvs_ref[...]).astype(kv_ref.dtype)


def project_part(slots, order, norm_gain, w_q, kv_weight, begun, scales, held=()):
    rows, depth = slots[0][0].shape
    tile = tile_of(depth, 512)
    q_cols, kv_cols = w_q.shape[1], kv_weight.shape[1]
    arrays = [array for slot in slots for array in slot]

    def whole(shape):
        return pl.BlockSpec(shape, lambda g, order: (0,) * len(shape))

    anywhere = pl.BlockSpec(memory_space=pl.ANY)
    operands = arrays + [norm_gain.reshape(1, -1)] + in_hbm([w_q, kv_weight])
    in_specs = [anywhere] * len(arrays) + [whole((1, norm_gain.shape[0])), anywhere, anywhere]
    sums = [(rows, q_cols), (rows, kv_cols), (rows, HEAD_SIZE)]
    if begun is not None:
        operands += list(begun)
        in_specs += [anywhere] * 3
    if scales is not None:
        operands += [scale.reshape(1, -1) for scale in scales]
        in_specs += [whole((1, q_cols)), whole((1, kv_cols))]
        out_shapes = [jax.ShapeDtypeStruct(shape, jnp.bfloat16) for shape in sums[:2]]
        scratch = [pltpu.VMEM(shape, jnp.float32) for shape in sums]
    else:
        out_shapes = [jax.ShapeDtypeStruct(shape, jnp.float32) for shape in sums]
        scratch = []
    kernel = functools.partial(
        qkv_kernel,
        [len(slot) for slot in slots],
        begun is not None,
        0 if scales is None else w_q.shape[0],
        tile,
    )
    return pl.pallas_call(
        without(kernel, 1 + len(operands), len(held)),
        grid_spec=pltpu.PrefetchScalarGridSpec(
            num_scalar_prefetch=1,
            grid=(1,),
            in_specs=in_specs + [anywhere] * len(held),
            out_specs=[whole(out.shape) for out in out_shapes],
            scratch_shapes=scratch
            + [pltpu.VMEM((rows, depth), jnp.bfloat16) for _ in arrays]
            + [
                pltpu.VMEM((WEIGHT_BUFFERS, tile, q_cols), jnp.bfloat16),
                pltpu.VMEM((WEIGHT_BUFFERS, tile, kv_cols), jnp.bfloat16),
                pltpu.SemaphoreType.DMA((len(arrays),)),
                pltpu.SemaphoreType.DMA((2, WEIGHT_BUFFERS)),
                pltpu.SemaphoreType.DMA((3,)),
            ],
        ),
        out_shape=out_shapes,
        compiler_params=pltpu.CompilerParams(vmem_limit_bytes=KERNEL_VMEM),
        cost_estimate=pl.CostEstimate(
            flops=2 * rows * depth * len(slots) * (q_cols + kv_cols) // COST_SHARE,
            bytes_accessed=(2 * depth * len(slots) * (q_cols + kv_cols)) // COST_SHARE,
            transcendentals=0,
        ),
        name="norm_qkv",
    )(order, *operands, *held)


def out_kernel(count, stacked, tile, order, x_ref, w_ref, *refs):
    if stacked:
        outs, refs = [refs[0].at[s] for s in range(count)], refs[1:]
    else:
        outs, refs = refs[:count], refs[count:]
    x_buf, w_buf, x_sem, w_sem, o_sem = refs[:5]
    o_bufs = refs[5:]
    per = o_bufs[0].shape[1] // tile
    steps = count * per
    ahead = min(steps, w_buf.shape[0])

    def weight_copy(step):
        at = pl.multiple_of((order[step // per] * per + lax.rem(step, per)) * tile, tile)
        buffer = lax.rem(step, ahead)
        return pltpu.make_async_copy(
            w_ref.at[:, pl.ds(at, tile)], w_buf.at[buffer], w_sem.at[buffer]
        )

    x_copy = pltpu.make_async_copy(x_ref, x_buf, x_sem)
    x_copy.start()
    for step in range(ahead):
        weight_copy(step).start()
    x_copy.wait()
    o_copies = []
    for s, (out, o_buf) in enumerate(zip(outs, o_bufs)):

        def body(j, carry, s=s, o_buf=o_buf):
            step = s * per + j
            weight_copy(step).wait()
            o_buf[:, pl.ds(pl.multiple_of(j * tile, tile), tile)] = jnp.dot(
                x_buf[...], w_buf[lax.rem(step, ahead)], preferred_element_type=jnp.float32
            ).astype(o_buf.dtype)

            @pl.when(step + ahead < steps)
            def _():
                weight_copy(step + ahead).start()

            return carry

        lax.fori_loop(0, per, body, 0)
        o_copies.append(pltpu.make_async_copy(o_buf, out, o_sem.at[s]))
        o_copies[-1].start()
    for copy in o_copies:
        copy.wait()


def project_out(attended, w_o, order, block, stacked=False, held=()):
    rows, depth = attended.shape
    tile = tile_of(block, 512)
    count = order.shape[0]
    anywhere = pl.BlockSpec(memory_space=pl.ANY)
    return pl.pallas_call(
        without(functools.partial(out_kernel, count, stacked, tile), 3, len(held)),
        grid_spec=pltpu.PrefetchScalarGridSpec(
            num_scalar_prefetch=1,
            grid=(1,),
            in_specs=[anywhere] * (2 + len(held)),
            out_specs=anywhere if stacked else [anywhere] * count,
            scratch_shapes=[
                pltpu.VMEM((rows, depth), jnp.bfloat16),
                pltpu.VMEM((WEIGHT_BUFFERS, depth, tile), jnp.bfloat16),
                pltpu.SemaphoreType.DMA,
                pltpu.SemaphoreType.DMA((WEIGHT_BUFFERS,)),
                pltpu.SemaphoreType.DMA((count,)),
            ]
            + [pltpu.VMEM((rows, block), jnp.bfloat16)] * count,
        ),
        out_shape=jax.ShapeDtypeStruct((count, rows, block), jnp.bfloat16)
        if stacked
        else [jax.ShapeDtypeStruct((rows, block), jnp.bfloat16)] * count,
        compiler_params=pltpu.CompilerParams(vmem_limit_bytes=KERNEL_VMEM),
        cost_estimate=pl.CostEstimate(
            flops=2 * rows * depth * count * block // COST_SHARE,
            bytes_accessed=(2 * depth * count * block) // COST_SHARE,
            transcendentals=0,
        ),
        name="project_out",
    )(order, attended, *in_hbm([w_o]), *held)


def with_ones(values):
    return jnp.concatenate([values, jnp.ones_like(values)], axis=1)


def scores_of(queries, keys):
    return lax.dot_general(
        queries, keys, (((1,), (1,)), ((), ())), preferred_element_type=jnp.float32
    )


def prefill_kernel(
    kv_heads, group, span, first, len_ref, q_ref, cache_ref, new_ref, o_ref, cache_buf, sem, *scratch
):
    accs, peaks = scratch[:kv_heads], scratch[kv_heads:]
    prompt = pl.program_id(0)

    def cache_copy(g):
        return pltpu.make_async_copy(cache_ref.at[0, first + g], cache_buf.at[g], sem.at[g])

    @pl.when(prompt == 0)
    def _():
        for g in range(cache_buf.shape[0]):
            cache_copy(g).start()

    tokens = q_ref.shape[0]
    rows = group * tokens
    live = len_ref[first + prompt]
    full = live // span
    query_token = lax.rem(lax.broadcasted_iota(jnp.int32, (rows, tokens), 0), tokens)
    key_token = lax.broadcasted_iota(jnp.int32, (rows, tokens), 1)
    causal = key_token <= query_token
    lane = lax.broadcasted_iota(jnp.int32, (1, span), 1)

    def queries_of(a):
        return jnp.concatenate(
            [
                q_ref[:, (a * group + h) * HEAD_SIZE : (a * group + h + 1) * HEAD_SIZE]
                for h in range(group)
            ],
            axis=0,
        )

    def columns(a, part):
        return pl.ds((2 * a + part) * HEAD_SIZE, HEAD_SIZE)

    for a in range(kv_heads):
        scores = jnp.where(causal, scores_of(queries_of(a), new_ref[:, columns(a, 0)]), MASKED)
        top = jnp.broadcast_to(jnp.max(scores, axis=-1, keepdims=True), (rows, HEAD_SIZE))
        weights = jnp.exp2(scores - top[:, :tokens]).astype(jnp.bfloat16)
        accs[a][...] = jnp.dot(
            weights, with_ones(new_ref[:, columns(a, 1)]), preferred_element_type=jnp.float32
        )
        peaks[a][...] = top

    cache_copy(prompt).wait()

    def block(s, bias):
        at = pl.multiple_of(s * span, span)
        scores = [
            scores_of(queries_of(a), cache_buf[prompt, pl.ds(at, span), columns(a, 0)])
            for a in range(kv_heads)
        ]
        for a in range(kv_heads):
            here = scores[a] if bias is None else scores[a] + bias
            before = peaks[a][...]
            top = jnp.maximum(before, jnp.max(here, axis=-1, keepdims=True))
            weights = jnp.exp2(
                here - jnp.concatenate([top] * (span // HEAD_SIZE), axis=1)
            ).astype(jnp.bfloat16)
            fade = jnp.exp2(before - top)
            values = cache_buf[prompt, pl.ds(at, span), columns(a, 1)]
            accs[a][...] = accs[a][...] * jnp.concatenate([fade, fade], axis=1) + jnp.dot(
                weights, with_ones(values), preferred_element_type=jnp.float32
            )
            peaks[a][...] = top

    def step(s, carry):
        block(s, None)
        return carry

    lax.fori_loop(0, full, step, 0)

    @pl.when(full * span < live)
    def _():
        block(full, jnp.where(lane + full * span < live, 0.0, MASKED))

    for a in range(kv_heads):
        result = accs[a][:, :HEAD_SIZE] / accs[a][:, HEAD_SIZE:]
        for h in range(group):
            o_ref[:, (a * group + h) * HEAD_SIZE : (a * group + h + 1) * HEAD_SIZE] = result[
                h * tokens : (h + 1) * tokens
            ].astype(o_ref.dtype)


def prefill_attention(queries, prefix_cache, first, count, new_kv, prefix_len):
    width = queries.shape[1]
    positions, page = prefix_cache.shape[2:]
    kv_heads = page // (2 * HEAD_SIZE)
    group = width // HEAD_SIZE // kv_heads
    span = tile_of(positions, 512)
    rows = group * PROMPT_TOKENS
    return pl.pallas_call(
        functools.partial(prefill_kernel, kv_heads, group, span, first),
        grid_spec=pltpu.PrefetchScalarGridSpec(
            num_scalar_prefetch=1,
            grid=(count,),
            in_specs=[
                pl.BlockSpec((PROMPT_TOKENS, width), lambda g, n: (g, 0)),
                pl.BlockSpec(memory_space=pl.ANY),
                pl.BlockSpec((PROMPT_TOKENS, page), lambda g, n: (g, 0)),
            ],
            out_specs=pl.BlockSpec((PROMPT_TOKENS, width), lambda g, n: (g, 0)),
            scratch_shapes=[
                pltpu.VMEM((count, positions, page), jnp.bfloat16),
                pltpu.SemaphoreType.DMA((count,)),
            ]
            + [pltpu.VMEM((rows, 2 * HEAD_SIZE), jnp.float32)] * kv_heads
            + [pltpu.VMEM((rows, HEAD_SIZE), jnp.float32)] * kv_heads,
        ),
        out_shape=jax.ShapeDtypeStruct((count * PROMPT_TOKENS, width), jnp.bfloat16),
        compiler_params=pltpu.CompilerParams(vmem_limit_bytes=KERNEL_VMEM),
        cost_estimate=pl.CostEstimate(
            flops=8 * count * rows * kv_heads * (positions + PROMPT_TOKENS) * HEAD_SIZE // COST_SHARE,
            bytes_accessed=(2 * count * positions * page) // COST_SHARE,
            transcendentals=count * rows * kv_heads * (positions + PROMPT_TOKENS),
        ),
        name="prefill_attention",
    )(prefix_len, queries, *in_hbm([prefix_cache]), new_kv)


def decode_kernel(
    kv_heads, batch, len_ref, row_ref, q_ref, cache_ref, landed_ref, fresh_ref, o_ref, acc, peak
):
    row_count, context = cache_ref.shape[1], cache_ref.shape[2]
    per_row = q_ref.shape[2]
    steps = fresh_ref.shape[1]
    rows = batch * per_row
    row_of = lax.broadcasted_iota(jnp.int32, (rows, batch * context), 0) // per_row
    key_row = lax.broadcasted_iota(jnp.int32, (rows, batch * context), 1) // context
    key_at = lax.rem(lax.broadcasted_iota(jnp.int32, (rows, batch * context), 1), context)
    fresh_query = lax.broadcasted_iota(jnp.int32, (rows, batch * steps), 0)
    fresh_key = lax.broadcasted_iota(jnp.int32, (rows, batch * steps), 1)
    fresh_live = (fresh_key // steps == fresh_query // per_row) & (
        lax.rem(fresh_key, steps) <= lax.rem(fresh_query, per_row) // (per_row // steps)
    )

    def cached(b, carry):
        first = b * batch
        live = jnp.zeros_like(key_row)
        for r in range(batch):
            live = jnp.where(key_row == r, len_ref[first + r], live)
        cache_live = (row_of == key_row) & (key_at < live)
        pages = cache_ref[0, pl.ds(first, batch)].reshape(batch * context, cache_ref.shape[3])
        fresh = fresh_ref[pl.ds(first, batch)].reshape(batch * steps, fresh_ref.shape[2])
        for a in range(kv_heads):
            queries = q_ref[pl.ds(first, batch), a].reshape(rows, HEAD_SIZE).astype(jnp.bfloat16)
            k_at, v_at = 2 * a * HEAD_SIZE, (2 * a + 1) * HEAD_SIZE
            scores = scores_of(queries, pages[:, k_at : k_at + HEAD_SIZE])
            scores = jnp.where(cache_live, scores, MASKED)
            recent = scores_of(queries, fresh[:, k_at : k_at + HEAD_SIZE].astype(jnp.bfloat16))
            recent = jnp.where(fresh_live, recent, MASKED)
            top = jnp.maximum(
                jnp.max(scores, axis=-1, keepdims=True), jnp.max(recent, axis=-1, keepdims=True)
            )
            weights = jnp.exp2(scores - top).astype(jnp.bfloat16)
            recent = jnp.exp2(recent - top).astype(jnp.bfloat16)
            total = jnp.dot(
                weights,
                with_ones(pages[:, v_at : v_at + HEAD_SIZE]),
                preferred_element_type=jnp.float32,
            ) + jnp.dot(
                recent,
                with_ones(fresh[:, v_at : v_at + HEAD_SIZE].astype(jnp.bfloat16)),
                preferred_element_type=jnp.float32,
            )
            acc[pl.ds(first, batch), a] = total.reshape(batch, per_row, 2 * HEAD_SIZE)
            peak[pl.ds(first, batch), a] = jnp.broadcast_to(top, (rows, HEAD_SIZE)).reshape(
                batch, per_row, HEAD_SIZE
            )
        return carry

    lax.fori_loop(0, row_count // batch, cached, 0)

    def arrival(slot, carry):
        row = row_ref[slot]

        @pl.when(row >= 0)
        def _():
            for a in range(kv_heads):
                queries = q_ref[row, a].astype(jnp.bfloat16)
                k_at, v_at = 2 * a * HEAD_SIZE, (2 * a + 1) * HEAD_SIZE
                scores = scores_of(queries, landed_ref[slot, :, k_at : k_at + HEAD_SIZE])
                before = peak[row, a]
                top = jnp.maximum(before, jnp.max(scores, axis=-1, keepdims=True))
                weights = jnp.exp2(scores - top[:, :1]).astype(jnp.bfloat16)
                fade = jnp.exp2(before - top)
                acc[row, a] = acc[row, a] * jnp.concatenate([fade, fade], axis=1) + jnp.dot(
                    weights,
                    with_ones(landed_ref[slot, :, v_at : v_at + HEAD_SIZE]),
                    preferred_element_type=jnp.float32,
                )

        return carry

    lax.fori_loop(0, row_ref.shape[0], arrival, 0)
    o_ref[...] = (acc[:, :, :, :HEAD_SIZE] / acc[:, :, :, HEAD_SIZE:]).astype(o_ref.dtype)


def decode_attention(queries, dec_cache, dec_len, landed, slot_rows, fresh, held=()):
    row_count, kv_heads, per_row = queries.shape[:3]
    context = dec_cache.shape[2]
    batch = max(1, min(row_count, 2 * HEAD_SIZE // context))
    whole = lambda array: pl.BlockSpec(array.shape, lambda g, *_: (0,) * array.ndim)
    return pl.pallas_call(
        without(functools.partial(decode_kernel, kv_heads, batch), 6, len(held)),
        grid_spec=pltpu.PrefetchScalarGridSpec(
            num_scalar_prefetch=2,
            grid=(1,),
            in_specs=[whole(queries), whole(dec_cache), whole(landed), whole(fresh)]
            + [pl.BlockSpec(memory_space=pl.ANY)] * len(held),
            out_specs=whole(queries),
            scratch_shapes=[
                pltpu.VMEM((row_count, kv_heads, per_row, 2 * HEAD_SIZE), jnp.float32),
                pltpu.VMEM((row_count, kv_heads, per_row, HEAD_SIZE), jnp.float32),
            ],
        ),
        out_shape=jax.ShapeDtypeStruct(queries.shape, jnp.float32),
        compiler_params=pltpu.CompilerParams(vmem_limit_bytes=KERNEL_VMEM),
        cost_estimate=pl.CostEstimate(
            flops=8 * queries.size * batch * context // COST_SHARE,
            bytes_accessed=(2 * dec_cache.size + 2 * landed.size) // COST_SHARE,
            transcendentals=queries.size * batch * context // HEAD_SIZE,
        ),
        name="decode_attention",
    )(dec_len, slot_rows, queries, dec_cache, landed, fresh, *held)


def shards(
    prefill_x,
    norm_gain,
    w_q,
    q_scale,
    key_value_weight,
    key_value_scale,
    w_o,
    o_scale,
    prefix_cache,
    prefix_len,
    dec_x,
    dec_cache,
    dec_len,
    place,
):
    prompts_total = prefix_cache.shape[1]
    row_count = dec_cache.shape[1]
    page_width = prefix_cache.shape[3]
    kv_heads = page_width // (2 * HEAD_SIZE)
    query_heads = w_q.shape[1] // HEAD_SIZE
    group_size = query_heads // kv_heads
    steps = dec_x.shape[0]
    section_count = lax.axis_size("section")
    section_index = lax.axis_index("section")
    tensor_count = lax.axis_size("tensor")
    tensor_index = lax.axis_index("tensor")
    head_span = max(1, 8 // query_heads)
    span_bits = head_span.bit_length() - 1
    block_width = w_o.shape[1] // tensor_count
    scales = (q_scale * EXP2_FACTOR, key_value_scale)

    weights = (norm_gain, w_q, key_value_weight)

    def kv_of_head(new_kv):
        for bit_number in range(span_bits):
            partner = partner_2(new_kv, "tensor", bit_number)
            new_kv = joined(new_kv, partner, bit_number, 1, tensor_index)
        return new_kv

    def finished(x, terms):
        total = sum(term.astype(jnp.float32) for term in terms)
        return (x.astype(jnp.float32) + total * o_scale).astype(jnp.bfloat16)

    dec_rows = dec_x.reshape(steps * row_count, -1)
    bounds = sorted({0, min(1, prompts_total - 1), prompts_total - 1, prompts_total})
    spans = list(zip(bounds[:-1], bounds[1:]))
    on_line = tensor_count == 4 and len(spans) == 3
    order = jnp.stack(
        line_order(tensor_index) if on_line else list(range(tensor_count))
    ).astype(jnp.int32)
    chunks = [prefill_x[first * PROMPT_TOKENS : last * PROMPT_TOKENS] for first, last in spans]
    blocks = chunks[:-1] + [jnp.concatenate([chunks[-1], dec_rows], axis=0)]
    pages = []

    def attention(k, queries):
        first, last = spans[k]
        return prefill_attention(queries, prefix_cache, first, last - first, pages[k], prefix_len)

    def keep(new_kv):
        new_kv = kv_of_head(new_kv)
        pages.append(new_kv[: chunks[len(pages)].shape[0]])
        return new_kv

    def back(attended, held=()):
        far, near, partner, own = project_out(
            attended, w_o, order[::-1], block_width, held=held
        )
        return LineScatter(own, partner, near, far, "tensor")

    def back_whole(attended):
        return project_out(
            attended, w_o, jnp.arange(tensor_count, dtype=jnp.int32), block_width, stacked=True
        )

    def summed(partial):
        return [lax.psum_scatter(partial, "tensor", scatter_dimension=0, tiled=False)]

    if on_line:
        first = LineGather(blocks[0], "tensor")
        first.second()
        begun = project_part(
            [[first.block], [first.partner]], order[:2], *weights, None, None, (first.middle,)
        )
        first.third(begun[2])
        second = LineGather(
            blocks[1], "tensor", (first.outer_far,), (first.outer, first.middle_far, begun[2])
        )
        queries, new_kv = project_part(first.slots()[2:], order[2:], *weights, begun, scales)
        keep(new_kv)
        attended = attention(0, queries)
        second.second(attended)
        sums = [back(attended, (second.partner, second.middle))]

        begun = project_part(
            [[second.block], [second.partner]], order[:2],
            *weights,
            None,
            None,
            (sums[0].own, second.outer),
        )
        second.third(begun[2])
        sums[0].second(begun[2])
        sums[0].third()
        third = LineGather(
            blocks[2], "tensor", (second.outer_far,), (second.outer, second.middle_far, begun[2])
        )
        queries, new_kv = project_part(
            second.slots()[2:], order[2:], *weights, begun, scales, sums[0].second_hop
        )
        keep(new_kv)
        third.second(queries)
        attended = attention(1, after(queries, third.partner, third.middle))
        third.third(attended)
        sums.append(back(attended, (third.outer, third.middle_far)))
        begun = project_part(
            [[third.block], [third.partner]],
            order[:2],
            *weights,
            None,
            None,
            (sums[1].own, *corners(sums[0].terms[1:])),
        )
        queries, new_kv = project_part(third.slots()[2:], order[2:], *weights, begun, scales)
        new_kv = keep(new_kv)
        sums[1].second(queries)
        sums[1].third_begin()
        sums.append(back(attention(2, after(queries, *sums[1].first_hop)), sums[1].second_hop))
        sums[1].third_start(sums[2].own)
        hold = (sums[2].own,)
    else:
        terms_of = []
        for k, block in enumerate(blocks):
            whole = lax.all_gather(block, "tensor", axis=1, tiled=True)
            queries, new_kv = project_part([[whole]], order[:1], *weights, None, scales)
            new_kv = keep(new_kv)
            terms_of.append(summed(back_whole(attention(k, queries))))
        hold = ()
    tokens = chunks[-1].shape[0]
    dec_queries, fresh_kv = queries[tokens:], new_kv[tokens:]

    own_block = after(jnp.concatenate(pages, axis=0), *hold).reshape(
        prompts_total, PROMPT_TOKENS, page_width
    )
    owners = (place // row_count).reshape(section_count, prompts_total)
    targets = (place % row_count).reshape(section_count, prompts_total)
    owner_hits = (owners[:, :, None] == jnp.arange(section_count)[None, None, :]).astype(jnp.int32)
    slot_ranks = jnp.sum((jnp.cumsum(owner_hits, axis=1) - owner_hits) * owner_hits, axis=2)
    capacity = prompts_total // 2
    slot_ids = jnp.arange(capacity)
    sending = lax.dynamic_index_in_dim(owner_hits, section_index, 0, keepdims=False)
    my_ranks = lax.dynamic_index_in_dim(slot_ranks, section_index, 0, keepdims=False)
    selector = (
        jnp.transpose(sending)[:, None, :] * (my_ranks[None, None, :] == slot_ids[None, :, None])
    ).astype(jnp.bfloat16)
    here = (owners == section_index)[:, None, :] & (
        slot_ranks[:, None, :] == slot_ids[None, :, None]
    )
    slot_rows = jnp.sum(jnp.where(here, targets[:, None, :] + 1, 0), axis=2) - 1
    outgoing = jnp.einsum(
        "skp,pcw->skcw", selector, own_block, preferred_element_type=jnp.float32
    ).astype(jnp.bfloat16)
    received = lax.all_to_all(outgoing, "section", split_axis=0, concat_axis=0, tiled=True)
    if on_line:
        sums[2].second(received)
        hold = (
            *sums[2].first_hop,
            *corners(sums[1].terms[1:]),
        )
    landed = received.reshape(section_count * capacity, PROMPT_TOKENS, page_width)

    dec_queries = jnp.transpose(
        dec_queries.reshape(steps, row_count, kv_heads, group_size, HEAD_SIZE), (1, 2, 0, 3, 4)
    ).reshape(row_count, kv_heads, steps * group_size, HEAD_SIZE)
    fresh = jnp.transpose(fresh_kv.reshape(steps, row_count, page_width), (1, 0, 2))
    dec_attended = decode_attention(
        dec_queries.astype(jnp.float32),
        dec_cache,
        dec_len,
        landed,
        slot_rows.reshape(-1).astype(jnp.int32),
        fresh.astype(jnp.float32),
        hold,
    )
    dec_attended = (
        jnp.transpose(
            dec_attended.reshape(row_count, kv_heads, steps, group_size, HEAD_SIZE), (2, 0, 1, 3, 4)
        )
        .reshape(steps * row_count, -1)
        .astype(jnp.bfloat16)
    )
    if on_line:
        to = [(tensor_index + shift) % tensor_count for shift in range(tensor_count)]
        sums[2].third(dec_attended)
        own, *parts = project_out(
            dec_attended,
            w_o,
            jnp.stack(to).astype(jnp.int32),
            block_width,
            held=sums[2].second_hop,
        )
        dec_terms = [own] + [
            lax.ppermute(
                part, "tensor", [(j, (j + shift) % tensor_count) for j in range(tensor_count)]
            )
            for shift, part in enumerate(parts, 1)
        ]
        terms_of = [each.terms for each in sums]
    else:
        dec_terms = summed(back_whole(dec_attended))
    prefill_out = jnp.concatenate(
        [finished(x, terms) for x, terms in zip(chunks, terms_of)], axis=0
    )
    decode_out = finished(dec_rows, dec_terms).reshape(dec_x.shape)
    return (prefill_out, decode_out)


def solution(mesh):
    in_specs = (
        P(("groups", "section"), "tensor"),
        P(),
        P(None, "tensor"),
        P("tensor"),
        P(None, "tensor"),
        P("tensor"),
        P("tensor", None),
        P("tensor"),
        P("tensor", ("groups", "section"), None, None),
        P(("groups", "section")),
        P(None, ("groups", "section"), "tensor"),
        P("tensor", ("groups", "section"), None, None),
        P(("groups", "section")),
        P("groups"),
    )
    out_specs = (P(("groups", "section"), "tensor"), P(None, ("groups", "section"), "tensor"))
    return jax.shard_map(shards, mesh=mesh, in_specs=in_specs, out_specs=out_specs, check_vma=False)
```

profile of v0, /device:TPU:12, one launch (start us, length us, event | category | flops | bytes accessed | tf_op | source)
XLA Modules:
  0.0 383.7 jit_solution(7093301102404465604)
XLA Ops:
  7.8 8.6 %collective-permute-done.1.refs_2_ = bf16[128,2048]{1,0:T(8,128)(2,1)S(1)} collective-permute-done((bf16[128,2048]{1,0:T(8,128)(2,1)S(1)}, bf16[128,2048]{1,0:T(8,128)(2,1)S(1)}, u32[]{:S(2)}, u32[]{:S(2)}) %collective-permute-start.1) | collective-permute-done | bytes 524320 | tf_op jit(solution)/shard_map/ppermute | solution.py:66
  24.5 8.3 %norm_qkv.6 = (f32[128,2048]{1,0:T(8,128)S(1)}, f32[128,512]{1,0:T(8,128)S(1)}, f32[128,128]{1,0:T(8,128)S(1)}) custom-call(s32[2]{0:T(128)S(1)} %pad_add_fusion.2.refs_0_, bf16[128,2048]{1,0:T(8,128)(2,1)S(1)} %get-tuple-element.122.refs_1_, bf16[128,2048]{1,0:T(8,128)(2,1)S(1)} %collective-permute-done.1.refs_2_, f32[1,8192]{1,0:T(1,128)S(1)} %bitcast.52, ...), custom_call_target="tpu_custom_call" | custom-call | flops 10485760 | bytes 81920 | tf_op jit(solution)/shard_map/norm_qkv/pallas_call | solution.py:244
  39.7 5.9 %collective-permute-done.4.refs_4_ = bf16[128,2048]{1,0:T(8,128)(2,1)S(1)} collective-permute-done((bf16[128,2048]{1,0:T(8,128)(2,1)S(1)}, bf16[128,2048]{1,0:T(8,128)(2,1)S(1)}, u32[]{:S(2)}, u32[]{:S(2)}) %collective-permute-start.4) | collective-permute-done | bytes 524320 | tf_op jit(solution)/shard_map/ppermute | solution.py:75
  55.4 8.6 %norm_qkv.7 = (bf16[128,2048]{1,0:T(8,128)(2,1)S(1)}, bf16[128,512]{1,0:T(8,128)(2,1)S(1)}) custom-call(s32[2]{0:T(128)S(1)} %pad_add_fusion.1.refs_0_, bf16[128,2048]{1,0:T(8,128)(2,1)S(1)} %copy-done.3, bf16[128,2048]{1,0:T(8,128)(2,1)S(1)} %copy-done.22, bf16[128,2048]{1,0:T(8,128)(2,1)S(1)} %copy-done.20, bf16[128,2048]{1,0:T(8,128)(2,1)S(1)} %copy-done.24, ...), custom_call_target="tpu_custom_call" | custom-call | flops 10485760 | bytes 81920 | tf_op jit(solution)/shard_map/norm_qkv/pallas_call | solution.py:244
  64.0 7.1 %prefill_attention.3.refs_1_ = bf16[128,2048]{1,0:T(8,128)(2,1)S(1)} custom-call(s32[4]{0:T(128)S(1)} %copy-done.38, bf16[128,2048]{1,0:T(8,128)(2,1)S(1)} %get-tuple-element.67.q_ref, bf16[1,4,2048,512]{3,2,1,0:T(8,128)(2,1)} %cache_ref.5, bf16[128,512]{1,0:T(8,128)(2,1)S(1)} %get-tuple-element.68.new_ref), custom_call_target="tpu_custom_call" | custom-call | flops 17825792 | bytes 8192 | tf_op jit(solution)/shard_map/prefill_attention/pallas_call | solution.py:453
  77.7 12.3 %project_out.4 = (bf16[128,2048]{1,0:T(8,128)(2,1)S(1)}, bf16[128,2048]{1,0:T(8,128)(2,1)S(1)}, bf16[128,2048]{1,0:T(8,128)(2,1)S(1)}, bf16[128,2048]{1,0:T(8,128)(2,1)S(1)}) custom-call(s32[4]{0:T(128)S(1)} %rev.2.refs_0_, bf16[128,2048]{1,0:T(8,128)(2,1)S(1)} %copy-done.7, bf16[2048,8192]{1,0:T(8,128)(2,1)} %refs_2_.7, ...), custom_call_target="tpu_custom_call" | custom-call | flops 16777216 | bytes 131072 | tf_op jit(solution)/shard_map/project_out/pallas_call | solution.py:323
  95.9 9.6 %norm_qkv.8 = (f32[256,2048]{1,0:T(8,128)S(1)}, f32[256,512]{1,0:T(8,128)S(1)}, f32[256,128]{1,0:T(8,128)S(1)}) custom-call(s32[2]{0:T(128)S(1)} %pad_add_fusion.2.refs_0_, bf16[256,2048]{1,0:T(8,128)(2,1)S(1)} %copy-done.1, bf16[256,2048]{1,0:T(8,128)(2,1)S(1)} %collective-permute-done.5.refs_3_.refs_2_, f32[1,8192]{1,0:T(1,128)S(1)} %bitcast.54, ...), custom_call_target="tpu_custom_call" | custom-call | flops 20971520 | bytes 81920 | tf_op jit(solution)/shard_map/norm_qkv/pallas_call | solution.py:244
  117.6 13.8 %collective-permute-done.14.refs_4_ = bf16[256,2048]{1,0:T(8,128)(2,1)S(1)} collective-permute-done((bf16[256,2048]{1,0:T(8,128)(2,1)}, bf16[256,2048]{1,0:T(8,128)(2,1)S(1)}, u32[]{:S(2)}, u32[]{:S(2)}) %collective-permute-start.14) | collective-permute-done | bytes 1048608 | tf_op jit(solution)/shard_map/ppermute | solution.py:75
  134.9 12.2 %norm_qkv.9 = (bf16[256,2048]{1,0:T(8,128)(2,1)S(1)}, bf16[256,512]{1,0:T(8,128)(2,1)S(1)}) custom-call(s32[2]{0:T(128)S(1)} %pad_add_fusion.1.refs_0_, bf16[256,2048]{1,0:T(8,128)(2,1)S(1)} %collective-permute-done.6.refs_4_.refs_1_, bf16[256,2048]{1,0:T(8,128)(2,1)S(1)} %collective-permute-done.8.refs_7_.refs_2_, ...), custom_call_target="tpu_custom_call" | custom-call | flops 20971520 | bytes 81920 | tf_op jit(solution)/shard_map/norm_qkv/pallas_call | solution.py:244
  154.7 14.5 %prefill_attention.4.refs_1_ = bf16[256,2048]{1,0:T(8,128)(2,1)S(1)} custom-call(s32[4]{0:T(128)S(1)} %copy-done.38, bf16[256,2048]{1,0:T(8,128)(2,1)S(1)} %get-tuple-element.88.q_ref, bf16[1,4,2048,512]{3,2,1,0:T(8,128)(2,1)} %cache_ref.5, bf16[256,512]{1,0:T(8,128)(2,1)S(1)} %get-tuple-element.89.new_ref), custom_call_target="tpu_custom_call" | custom-call | flops 35651584 | bytes 16384 | tf_op jit(solution)/shard_map/prefill_attention/pallas_call | solution.py:453
  170.7 13.8 %project_out.5 = (bf16[256,2048]{1,0:T(8,128)(2,1)}, bf16[256,2048]{1,0:T(8,128)(2,1)}, bf16[256,2048]{1,0:T(8,128)(2,1)S(1)}, bf16[256,2048]{1,0:T(8,128)(2,1)S(1)}) custom-call(s32[4]{0:T(128)S(1)} %rev.2.refs_0_, bf16[256,2048]{1,0:T(8,128)(2,1)S(1)} %prefill_attention.4.refs_1_, bf16[2048,8192]{1,0:T(8,128)(2,1)} %refs_2_.7, ...), custom_call_target="tpu_custom_call" | custom-call | flops 33554432 | bytes 131072 | tf_op jit(solution)/shard_map/project_out/pallas_call | solution.py:323
  186.8 6.4 %collective-permute-start.20 = (bf16[192,2048]{1,0:T(8,128)(2,1)}, bf16[192,2048]{1,0:T(8,128)(2,1)}, u32[]{:S(2)}, u32[]{:S(2)}) collective-permute-start(bf16[192,2048]{1,0:T(8,128)(2,1)} %collective-permute-done.18.refs_4_.refs_3_), channel_id=1, source_target_pairs={{4,0},{8,12},{5,1},{9,13},{6,2},{10,14},{7,3},{11,15},{20,16},{24,... | collective-permute-start | bytes 2359304 | tf_op jit(solution)/shard_map/ppermute | solution.py:75
  196.3 8.5 %collective-permute-done.11 = bf16[128,2048]{1,0:T(8,128)(2,1)} collective-permute-done((bf16[128,2048]{1,0:T(8,128)(2,1)S(1)}, bf16[128,2048]{1,0:T(8,128)(2,1)}, u32[]{:S(2)}, u32[]{:S(2)}) %collective-permute-start.11) | collective-permute-done | bytes 524320 | tf_op jit(solution)/shard_map/ppermute | solution.py:119
  205.6 14.8 %collective-permute-done.12 = bf16[128,2048]{1,0:T(8,128)(2,1)} collective-permute-done((bf16[128,2048]{1,0:T(8,128)(2,1)}, bf16[128,2048]{1,0:T(8,128)(2,1)}, u32[]{:S(2)}, u32[]{:S(2)}) %collective-permute-start.12) | collective-permute-done | bytes 524320 | tf_op jit(solution)/shard_map/ppermute | solution.py:120
  222.3 8.4 %norm_qkv.10 = (f32[192,2048]{1,0:T(8,128)S(1)}, f32[192,512]{1,0:T(8,128)S(1)}, f32[192,128]{1,0:T(8,128)S(1)}) custom-call(s32[2]{0:T(128)S(1)} %pad_add_fusion.2.refs_0_, bf16[192,2048]{1,0:T(8,128)(2,1)S(1)} %pad_maximum_fusion.1.refs_1_, bf16[192,2048]{1,0:T(8,128)(2,1)S(1)} %copy-done.18, f32[1,8192]{1,0:T(1,128)S(1)} %bitcast.56, ...), custom_call_target="tpu_custom_call" | custom-call | flops 15728640 | bytes 81920 | tf_op jit(solution)/shard_map/norm_qkv/pallas_call | solution.py:244
  230.7 11.7 %norm_qkv.11 = (bf16[192,2048]{1,0:T(8,128)(2,1)S(1)}, bf16[192,512]{1,0:T(8,128)(2,1)S(1)}) custom-call(s32[2]{0:T(128)S(1)} %pad_add_fusion.1.refs_0_, bf16[192,2048]{1,0:T(8,128)(2,1)S(1)} %copy-done.16, bf16[192,2048]{1,0:T(8,128)(2,1)S(1)} %collective-permute-done.17.refs_3_.refs_2_, bf16[192,2048]{1,0:T(8,128)(2,1)} %collective-permute-done.18.refs_4_.refs_3_, ...), custom_call_target="tpu_custom_call" | custom-call | flops 15728640 | bytes 81920 | tf_op jit(solution)/shard_map/norm_qkv/pallas_call | solution.py:244
  251.2 5.6 %prefill_attention.5.refs_1_ = bf16[128,2048]{1,0:T(8,128)(2,1)S(1)} custom-call(s32[4]{0:T(128)S(1)} %copy-done.38, bf16[192,2048]{1,0:T(8,128)(2,1)S(1)} %get-tuple-element.103.q_ref, bf16[1,4,2048,512]{3,2,1,0:T(8,128)(2,1)} %cache_ref.5, bf16[128,512]{1,0:T(8,128)(2,1)S(1)} %slice.43.new_ref), custom_call_target="tpu_custom_call" | custom-call | flops 17825792 | bytes 8192 | tf_op jit(solution)/shard_map/prefill_attention/pallas_call | solution.py:453
  256.8 11.6 %collective-permute-done.21 = bf16[256,2048]{1,0:T(8,128)(2,1)} collective-permute-done((bf16[256,2048]{1,0:T(8,128)(2,1)}, bf16[256,2048]{1,0:T(8,128)(2,1)}, u32[]{:S(2)}, u32[]{:S(2)}) %collective-permute-start.21) | collective-permute-done | bytes 1048608 | tf_op jit(solution)/shard_map/ppermute | solution.py:104
  271.5 12.5 %project_out.6 = (bf16[128,2048]{1,0:T(8,128)(2,1)}, bf16[128,2048]{1,0:T(8,128)(2,1)S(1)}, bf16[128,2048]{1,0:T(8,128)(2,1)S(1)}, bf16[128,2048]{1,0:T(8,128)(2,1)S(1)}) custom-call(s32[4]{0:T(128)S(1)} %rev.2.refs_0_, bf16[128,2048]{1,0:T(8,128)(2,1)S(1)} %prefill_attention.5.refs_1_, bf16[2048,8192]{1,0:T(8,128)(2,1)} %refs_2_.7, ...), custom_call_target="tpu_custom_call" | custom-call | flops 16777216 | bytes 131072 | tf_op jit(solution)/shard_map/project_out/pallas_call | solution.py:323
  301.1 7.1 %all-to-all-done = bf16[4,2,128,512]{3,2,1,0:T(8,128)(2,1)} async-done(((bf16[4,2,128,512]{3,2,1,0:T(8,128)(2,1)}), bf16[4,2,128,512]{3,2,1,0:T(8,128)(2,1)}, u32[]{:S(2)}, u32[]{:S(2)}) %all-to-all-start) | async-done | bytes 1048608 | tf_op jit(solution)/shard_map/all_to_all | solution.py:751
  315.4 6.5 %collective-permute-done.23 = bf16[256,2048]{1,0:T(8,128)(2,1)} collective-permute-done((bf16[256,2048]{1,0:T(8,128)(2,1)S(1)}, bf16[256,2048]{1,0:T(8,128)(2,1)}, u32[]{:S(2)}, u32[]{:S(2)}) %collective-permute-start.23) | collective-permute-done | bytes 1048608 | tf_op jit(solution)/shard_map/ppermute | solution.py:119
  324.8 8.5 %decode_attention.1 = f32[32,2,16,128]{3,2,1,0:T(8,128)S(1)} custom-call(s32[32]{0:T(128)S(1)} %copy-done.39, s32[8]{0:T(128)S(1)} %sub.15.refs_1_, f32[32,2,16,128]{3,2,1,0:T(8,128)S(1)} %bitcast.51, bf16[1,32,64,512]{3,2,1,0:T(8,128)(2,1)S(1)} %copy-done.8, bf16[8,128,512]{2,1,0:T(8,128)(2,1)} %bitcast.17.refs_4_, f32[32,2,512]{2,1,0:T(2,128)S(1)} %bitcast.58, ...), custom_call_target="tpu_custom_call" | custom-call | flops 1048576 | bytes 12288 | tf_op jit(solution)/shard_map/decode_attention/pallas_call | solution.py:565
  340.6 12.3 %project_out.7 = (bf16[64,2048]{1,0:T(8,128)(2,1)S(1)}, bf16[64,2048]{1,0:T(8,128)(2,1)S(1)}, bf16[64,2048]{1,0:T(8,128)(2,1)S(1)}, bf16[64,2048]{1,0:T(8,128)(2,1)S(1)}) custom-call(s32[4]{0:T(128)S(1)} %pad_add_fusion.3.refs_0_, bf16[64,2048]{1,0:T(8,128)(2,1)S(1)} %convert_element_type.239.refs_1_, bf16[2048,8192]{1,0:T(8,128)(2,1)} %refs_2_.7, ...), custom_call_target="tpu_custom_call" | custom-call | flops 8388608 | bytes 131072 | tf_op jit(solution)/shard_map/project_out/pallas_call | solution.py:323
  362.2 13.2 %collective-permute-done.31 = bf16[64,2048]{1,0:T(8,128)(2,1)S(1)} collective-permute-done((bf16[64,2048]{1,0:T(8,128)(2,1)S(1)}, bf16[64,2048]{1,0:T(8,128)(2,1)S(1)}, u32[]{:S(2)}, u32[]{:S(2)}) %collective-permute-start.31) | collective-permute-done | bytes 262176 | tf_op jit(solution)/shard_map/ppermute | solution.py:791
  (206 shorter events, 139.6 us)
Async XLA Ops:
  36.4 35.6 %collective-permute-start.6 = (bf16[256,2048]{1,0:T(8,128)(2,1)S(1)}, bf16[256,2048]{1,0:T(8,128)(2,1)S(1)}, u32[]{:S(2)}, u32[]{:S(2)}) collective-permute-start(bf16[256,2048]{1,0:T(8,128)(2,1)S(1)} %slice.39.refs_1_), channel_id=1, source_target_pairs={{4,8},{8,4},{5,9},{9,5},{6,10},{10,6},{7,11},{11,7},{20,24},{24,20... | collective-permute-start | bytes 3145736 | tf_op jit(solution)/shard_map/ppermute | solution.py:67
  46.5 25.5 %collective-permute-start.5 = (bf16[256,2048]{1,0:T(8,128)(2,1)S(1)}, bf16[256,2048]{1,0:T(8,128)(2,1)S(1)}, u32[]{:S(2)}, u32[]{:S(2)}) collective-permute-start(bf16[256,2048]{1,0:T(8,128)(2,1)S(1)} %slice.39.refs_1_), channel_id=1, source_target_pairs={{0,4},{4,0},{8,12},{12,8},{1,5},{5,1},{9,13},{13,9},{2,6},{6,2},{1... | collective-permute-start | bytes 3145736 | tf_op jit(solution)/shard_map/ppermute | solution.py:66
  71.9 24.0 %collective-permute-start.8 = (bf16[256,2048]{1,0:T(8,128)(2,1)S(1)}, bf16[256,2048]{1,0:T(8,128)(2,1)S(1)}, u32[]{:S(2)}, u32[]{:S(2)}) collective-permute-start(bf16[256,2048]{1,0:T(8,128)(2,1)S(1)} %collective-permute-done.6.refs_4_.refs_1_), channel_id=1, source_target_pairs={{4,0},{8,12},{5,1},{9,13},{6,2},{10,14},{7,3},{11,15},{20,16},{24,... | collective-permute-start | bytes 3145736 | tf_op jit(solution)/shard_map/ppermute | solution.py:71
  74.0 31.6 %collective-permute-start.13 = (bf16[256,2048]{1,0:T(8,128)(2,1)S(1)}, bf16[256,2048]{1,0:T(8,128)(2,1)}, u32[]{:S(2)}, u32[]{:S(2)}) collective-permute-start(bf16[256,2048]{1,0:T(8,128)(2,1)S(1)} %collective-permute-done.5.refs_3_.refs_2_), channel_id=1, source_target_pairs={{4,8},{8,4},{5,9},{9,5},{6,10},{10,6},{7,11},{11,7},{20,24},{24,20... | collective-permute-start | bytes 3145736 | tf_op jit(solution)/shard_map/ppermute | solution.py:72
  90.0 20.1 %collective-permute-start.7 = (bf16[128,2048]{1,0:T(8,128)(2,1)S(1)}, bf16[128,2048]{1,0:T(8,128)(2,1)S(1)}, u32[]{:S(2)}, u32[]{:S(2)}) collective-permute-start(bf16[128,2048]{1,0:T(8,128)(2,1)S(1)} %get-tuple-element.73), channel_id=1, source_target_pairs={{0,4},{12,8},{1,5},{13,9},{2,6},{14,10},{3,7},{15,11},{16,20},{28,... | collective-permute-start | bytes 1572872 | tf_op jit(solution)/shard_map/ppermute | solution.py:99
  105.6 25.8 %collective-permute-start.14 = (bf16[256,2048]{1,0:T(8,128)(2,1)}, bf16[256,2048]{1,0:T(8,128)(2,1)S(1)}, u32[]{:S(2)}, u32[]{:S(2)}) collective-permute-start(bf16[256,2048]{1,0:T(8,128)(2,1)} %collective-permute-done.13.refs_3_), channel_id=1, source_target_pairs={{4,0},{8,12},{5,1},{9,13},{6,2},{10,14},{7,3},{11,15},{20,16},{24,... | collective-permute-start | bytes 3145736 | tf_op jit(solution)/shard_map/ppermute | solution.py:75
  110.2 23.6 %collective-permute-start.9 = (bf16[128,2048]{1,0:T(8,128)(2,1)S(1)}, bf16[128,2048]{1,0:T(8,128)(2,1)S(1)}, u32[]{:S(2)}, u32[]{:S(2)}) collective-permute-start(bf16[128,2048]{1,0:T(8,128)(2,1)S(1)} %get-tuple-element.76), channel_id=1, source_target_pairs={{0,4},{12,8},{1,5},{13,9},{2,6},{14,10},{3,7},{15,11},{16,20},{28,... | collective-permute-start | bytes 1572872 | tf_op jit(solution)/shard_map/ppermute | solution.py:104
  111.5 22.4 %collective-permute-start.10 = (bf16[128,2048]{1,0:T(8,128)(2,1)S(1)}, bf16[128,2048]{1,0:T(8,128)(2,1)S(1)}, u32[]{:S(2)}, u32[]{:S(2)}) collective-permute-start(bf16[128,2048]{1,0:T(8,128)(2,1)S(1)} %add_convert_fusion.11), channel_id=1, source_target_pairs={{4,8},{8,4},{5,9},{9,5},{6,10},{10,6},{7,11},{11,7},{20,24},{24,20... | collective-permute-start | bytes 1572872 | tf_op jit(solution)/shard_map/ppermute | solution.py:105
  113.7 33.4 %collective-permute-start.16 = (bf16[192,2048]{1,0:T(8,128)(2,1)S(1)}, bf16[192,2048]{1,0:T(8,128)(2,1)S(1)}, u32[]{:S(2)}, u32[]{:S(2)}) collective-permute-start(bf16[192,2048]{1,0:T(8,128)(2,1)S(1)} %pad_maximum_fusion.1.refs_1_), channel_id=1, source_target_pairs={{4,8},{8,4},{5,9},{9,5},{6,10},{10,6},{7,11},{11,7},{20,24},{24,20... | collective-permute-start | bytes 2359304 | tf_op jit(solution)/shard_map/ppermute | solution.py:67
  149.1 20.2 %collective-permute-start.17 = (bf16[192,2048]{1,0:T(8,128)(2,1)S(1)}, bf16[192,2048]{1,0:T(8,128)(2,1)S(1)}, u32[]{:S(2)}, u32[]{:S(2)}) collective-permute-start(bf16[192,2048]{1,0:T(8,128)(2,1)S(1)} %collective-permute-done.16.refs_1_), channel_id=1, source_target_pairs={{4,0},{8,12},{5,1},{9,13},{6,2},{10,14},{7,3},{11,15},{20,16},{24,... | collective-permute-start | bytes 2359304 | tf_op jit(solution)/shard_map/ppermute | solution.py:71
  185.5 56.9 %collective-permute-start.19 = (bf16[256,2048]{1,0:T(8,128)(2,1)}, bf16[256,2048]{1,0:T(8,128)(2,1)}, u32[]{:S(2)}, u32[]{:S(2)}) collective-permute-start(bf16[256,2048]{1,0:T(8,128)(2,1)} %get-tuple-element.94), channel_id=1, source_target_pairs={{0,4},{12,8},{1,5},{13,9},{2,6},{14,10},{3,7},{15,11},{16,20},{28,... | collective-permute-start | bytes 3145736 | tf_op jit(solution)/shard_map/ppermute | solution.py:99
  186.8 43.9 %collective-permute-start.20 = (bf16[192,2048]{1,0:T(8,128)(2,1)}, bf16[192,2048]{1,0:T(8,128)(2,1)}, u32[]{:S(2)}, u32[]{:S(2)}) collective-permute-start(bf16[192,2048]{1,0:T(8,128)(2,1)} %collective-permute-done.18.refs_4_.refs_3_), channel_id=1, source_target_pairs={{4,0},{8,12},{5,1},{9,13},{6,2},{10,14},{7,3},{11,15},{20,16},{24,... | collective-permute-start | bytes 2359304 | tf_op jit(solution)/shard_map/ppermute | solution.py:75
  196.0 24.4 %collective-permute-start.12 = (bf16[128,2048]{1,0:T(8,128)(2,1)}, bf16[128,2048]{1,0:T(8,128)(2,1)}, u32[]{:S(2)}, u32[]{:S(2)}) collective-permute-start(bf16[128,2048]{1,0:T(8,128)(2,1)} %add_convert_fusion.9.refs_14_), channel_id=1, source_target_pairs={{0,4},{4,0},{8,12},{12,8},{1,5},{5,1},{9,13},{13,9},{2,6},{6,2},{1... | collective-permute-start | bytes 1572872 | tf_op jit(solution)/shard_map/ppermute | solution.py:120
  245.7 22.7 %collective-permute-start.21 = (bf16[256,2048]{1,0:T(8,128)(2,1)}, bf16[256,2048]{1,0:T(8,128)(2,1)}, u32[]{:S(2)}, u32[]{:S(2)}) collective-permute-start(bf16[256,2048]{1,0:T(8,128)(2,1)} %get-tuple-element.100), channel_id=1, source_target_pairs={{0,4},{12,8},{1,5},{13,9},{2,6},{14,10},{3,7},{15,11},{16,20},{28,... | collective-permute-start | bytes 3145736 | tf_op jit(solution)/shard_map/ppermute | solution.py:104
  247.4 23.6 %collective-permute-start.22 = (bf16[256,2048]{1,0:T(8,128)(2,1)}, bf16[256,2048]{1,0:T(8,128)(2,1)S(1)}, u32[]{:S(2)}, u32[]{:S(2)}) collective-permute-start(bf16[256,2048]{1,0:T(8,128)(2,1)} %add_convert_fusion.3), channel_id=1, source_target_pairs={{4,8},{8,4},{5,9},{9,5},{6,10},{10,6},{7,11},{11,7},{20,24},{24,20... | collective-permute-start | bytes 3145736 | tf_op jit(solution)/shard_map/ppermute | solution.py:105
  289.5 18.8 %all-to-all-start = ((bf16[4,2,128,512]{3,2,1,0:T(8,128)(2,1)}), bf16[4,2,128,512]{3,2,1,0:T(8,128)(2,1)}, u32[]{:S(2)}, u32[]{:S(2)}) async-start(bf16[4,2,128,512]{3,2,1,0:T(8,128)(2,1)} %copy.35), calls=%async_computation | async-start | bytes 2097152 | tf_op jit(solution)/shard_map/all_to_all | solution.py:751
  293.9 28.1 %collective-permute-start.23 = (bf16[256,2048]{1,0:T(8,128)(2,1)S(1)}, bf16[256,2048]{1,0:T(8,128)(2,1)}, u32[]{:S(2)}, u32[]{:S(2)}) collective-permute-start(bf16[256,2048]{1,0:T(8,128)(2,1)S(1)} %add_convert_fusion.2.refs_3_), channel_id=1, source_target_pairs={{4,8},{8,4},{5,9},{9,5},{6,10},{10,6},{7,11},{11,7},{20,24},{24,20... | collective-permute-start | bytes 3145736 | tf_op jit(solution)/shard_map/ppermute | solution.py:119
  297.8 26.2 %collective-permute-start.24 = (bf16[256,2048]{1,0:T(8,128)(2,1)S(1)}, bf16[256,2048]{1,0:T(8,128)(2,1)}, u32[]{:S(2)}, u32[]{:S(2)}) collective-permute-start(bf16[256,2048]{1,0:T(8,128)(2,1)S(1)} %add_convert_fusion.1.refs_4_), channel_id=1, source_target_pairs={{0,4},{4,0},{8,12},{12,8},{1,5},{5,1},{9,13},{13,9},{2,6},{6,2},{1... | collective-permute-start | bytes 3145736 | tf_op jit(solution)/shard_map/ppermute | solution.py:120
  308.2 26.2 %collective-permute-start.26 = (bf16[128,2048]{1,0:T(8,128)(2,1)}, bf16[128,2048]{1,0:T(8,128)(2,1)}, u32[]{:S(2)}, u32[]{:S(2)}) collective-permute-start(bf16[128,2048]{1,0:T(8,128)(2,1)} %copy-done.31), channel_id=1, source_target_pairs={{0,4},{12,8},{1,5},{13,9},{2,6},{14,10},{3,7},{15,11},{16,20},{28,... | collective-permute-start | bytes 1572872 | tf_op jit(solution)/shard_map/ppermute | solution.py:104
  311.4 24.2 %collective-permute-start.27 = (bf16[128,2048]{1,0:T(8,128)(2,1)}, bf16[128,2048]{1,0:T(8,128)(2,1)}, u32[]{:S(2)}, u32[]{:S(2)}) collective-permute-start(bf16[128,2048]{1,0:T(8,128)(2,1)} %add_convert_fusion.7.refs_6_), channel_id=1, source_target_pairs={{4,8},{8,4},{5,9},{9,5},{6,10},{10,6},{7,11},{11,7},{20,24},{24,20... | collective-permute-start | bytes 1572872 | tf_op jit(solution)/shard_map/ppermute | solution.py:105
  336.9 43.0 %collective-permute-start.28 = (bf16[128,2048]{1,0:T(8,128)(2,1)S(1)}, bf16[128,2048]{1,0:T(8,128)(2,1)S(1)}, u32[]{:S(2)}, u32[]{:S(2)}) collective-permute-start(bf16[128,2048]{1,0:T(8,128)(2,1)S(1)} %add_convert_fusion.6.refs_3_), channel_id=1, source_target_pairs={{4,8},{8,4},{5,9},{9,5},{6,10},{10,6},{7,11},{11,7},{20,24},{24,20... | collective-permute-start | bytes 1572872 | tf_op jit(solution)/shard_map/ppermute | solution.py:119
  340.6 39.3 %collective-permute-start.29 = (bf16[128,2048]{1,0:T(8,128)(2,1)S(1)}, bf16[128,2048]{1,0:T(8,128)(2,1)S(1)}, u32[]{:S(2)}, u32[]{:S(2)}) collective-permute-start(bf16[128,2048]{1,0:T(8,128)(2,1)S(1)} %add_convert_fusion.5.refs_4_), channel_id=1, source_target_pairs={{0,4},{4,0},{8,12},{12,8},{1,5},{5,1},{9,13},{13,9},{2,6},{6,2},{1... | collective-permute-start | bytes 1572872 | tf_op jit(solution)/shard_map/ppermute | solution.py:120
  353.4 22.1 %collective-permute-start.31 = (bf16[64,2048]{1,0:T(8,128)(2,1)S(1)}, bf16[64,2048]{1,0:T(8,128)(2,1)S(1)}, u32[]{:S(2)}, u32[]{:S(2)}) collective-permute-start(bf16[64,2048]{1,0:T(8,128)(2,1)S(1)} %get-tuple-element.118), channel_id=1, source_target_pairs={{0,8},{4,12},{8,0},{12,4},{1,9},{5,13},{9,1},{13,5},{2,10},{6,14},... | collective-permute-start | bytes 786440 | tf_op jit(solution)/shard_map/ppermute | solution.py:791
  357.4 21.6 %collective-permute-start.32 = (bf16[64,2048]{1,0:T(8,128)(2,1)S(1)}, bf16[64,2048]{1,0:T(8,128)(2,1)S(1)}, u32[]{:S(2)}, u32[]{:S(2)}) collective-permute-start(bf16[64,2048]{1,0:T(8,128)(2,1)S(1)} %get-tuple-element.119), channel_id=1, source_target_pairs={{0,12},{4,0},{8,4},{12,8},{1,13},{5,1},{9,5},{13,9},{2,14},{6,2},{... | collective-permute-start | bytes 786440 | tf_op jit(solution)/shard_map/ppermute | solution.py:791
  (58 other events, 680.7 us)
where the time goes:
time: 390 us; the launch traced here: 384 us
  Pallas kernels  146 us (37%)
  waiting for transfers between devices  111 us (28%)
  starting transfers between devices  82.4 us (21%)
  local copies, waits for them, and re-layouts  21.7 us (6%)
  other arithmetic  20 us (5%)
    pallas_call x6, Pallas kernels, project_part(): pl.pallas_call(without(kernel, 1 + len(operands), len(held)), grid_spec=p...  58.9 us
    pallas_call x4, Pallas kernels, project_out(): pl.pallas_call(without(functools.partial(out_kernel, count, stacked, tile...  50.9 us
    pallas_call x3, Pallas kernels, prefill_attention(): pl.pallas_call(functools.partial(prefill_kernel, kv_heads, group, span, f...  27.2 us
    ppermute x3, waiting for transfers between devices, third(): lax.ppermute(after(self.middle_far, *held), self.axis, OUTWARD)  19.7 us
    ppermute x3, waiting for transfers between devices, shards(): lax.ppermute(part, 'tensor', [(j, (j + shift) % tensor_count) for j in ra...  19.2 us
    ppermute x3, waiting for transfers between devices, third_start(): partner = lax.ppermute(partner, self.axis, OUTER)  16.1 us
    ppermute x3, waiting for transfers between devices, third_start(): near = lax.ppermute(near, self.axis, MIDDLE)  15 us
    unnamed x97, local copies, waits for them, and re-layouts  14.5 us
  transfers between devices with their start and end apart: 34, of which 19 were waited for; matrix products, arithmetic and copies ran while one was open for 5% of the time, Pallas kernels for 31%

commit v1 on v0

--- a/solution.py
+++ b/solution.py
@@ -639,6 +639,11 @@
     ).astype(jnp.int32)
     chunks = [prefill_x[first * PROMPT_TOKENS : last * PROMPT_TOKENS] for first, last in spans]
     blocks = chunks[:-1] + [jnp.concatenate([chunks[-1], dec_rows], axis=0)]
+    if on_line:
+        begin = chunks[0].shape[0]
+        rest, dec_rest = after_all((prefill_x[begin:], dec_rows), blocks[0])
+        blocks[1] = rest[: chunks[1].shape[0]]
+        blocks[2] = jnp.concatenate([rest[chunks[1].shape[0] :], dec_rest], axis=0)
     pages = []
 
     def attention(k, queries):
@@ -707,9 +712,11 @@
             *weights,
             None,
             None,
-            (sums[1].own, *corners(sums[0].terms[1:])),
-        )
-        queries, new_kv = project_part(third.slots()[2:], order[2:], *weights, begun, scales)
+            (sums[1].own,),
+        )
+        queries, new_kv = project_part(
+            third.slots()[2:], order[2:], *weights, begun, scales, sums[0].terms[1:]
+        )
         new_kv = keep(new_kv)
         sums[1].second(queries)
         sums[1].third_begin()
@@ -751,10 +758,7 @@
     received = lax.all_to_all(outgoing, "section", split_axis=0, concat_axis=0, tiled=True)
     if on_line:
         sums[2].second(received)
-        hold = (
-            *sums[2].first_hop,
-            *corners(sums[1].terms[1:]),
-        )
+        hold = sums[2].first_hop
     landed = received.reshape(section_count * capacity, PROMPT_TOKENS, page_width)
 
     dec_queries = jnp.transpose(
@@ -785,7 +789,7 @@
             w_o,
             jnp.stack(to).astype(jnp.int32),
             block_width,
-            held=sums[2].second_hop,
+            held=(*sums[2].second_hop, *corners(sums[1].terms[1:])),
         )
         dec_terms = [own] + [
             lax.ppermute(

time: 390 us -> 377 us (0.967)
  waiting for transfers between devices: 111 us -> 98.3 us
    ppermute x3, waiting for transfers between devices: 15 us -> 0.01 us  [third_start(): near = lax.ppermute(near, self.axis, MIDDLE)]
    ppermute x3, waiting for transfers between devices: 12.6 us -> 16.9 us  [second(): self.near_in = lax.ppermute(near, self.axis, INWARD)]
    unnamed x97 -> x103, local copies, waits for them, and re-layouts: 14.5 us -> 16.1 us
  transfers between devices with their start and end apart: 34 -> 34, of which waited for: 19 -> 16; matrix products, arithmetic and copies ran while one was open for 5% -> 5% of each run, Pallas kernels for 31% -> 32%
where the time goes in v1:
time: 377 us; the launch traced here: 371 us
  Pallas kernels  144 us (38%)
  waiting for transfers between devices  98.3 us (26%)
  starting transfers between devices  82.8 us (22%)
  local copies, waits for them, and re-layouts  21.8 us (6%)
  other arithmetic  21.8 us (6%)
    pallas_call x6, Pallas kernels, project_part(): pl.pallas_call(without(kernel, 1 + len(operands), len(held)), grid_spec=p...  58.9 us
    pallas_call x4, Pallas kernels, project_out(): pl.pallas_call(without(functools.partial(out_kernel, count, stacked, tile...  50.9 us
    pallas_call x3, Pallas kernels, prefill_attention(): pl.pallas_call(functools.partial(prefill_kernel, kv_heads, group, span, f...  23.9 us
    ppermute x3, waiting for transfers between devices, third(): lax.ppermute(after(self.middle_far, *held), self.axis, OUTWARD)  19.3 us
    ppermute x3, waiting for transfers between devices, shards(): lax.ppermute(part, 'tensor', [(j, (j + shift) % tensor_count) for j in ra...  19.1 us
    ppermute x3, waiting for transfers between devices, second(): self.near_in = lax.ppermute(near, self.axis, INWARD)  16.9 us
    unnamed x103, local copies, waits for them, and re-layouts  16.1 us
    ppermute x3, waiting for transfers between devices, third_start(): partner = lax.ppermute(partner, self.axis, OUTER)  14 us
  transfers between devices with their start and end apart: 34, of which 16 were waited for; matrix products, arithmetic and copies ran while one was open for 5% of the time, Pallas kernels for 32%

profile of v1, /device:TPU:12, one launch (start us, length us, event | category | flops | bytes accessed | tf_op | source)
XLA Modules:
  0.0 371.2 jit_solution(8836311895536684810)
XLA Ops:
  6.8 8.6 %collective-permute-done.1.refs_2_ = bf16[128,2048]{1,0:T(8,128)(2,1)S(1)} collective-permute-done((bf16[128,2048]{1,0:T(8,128)(2,1)S(1)}, bf16[128,2048]{1,0:T(8,128)(2,1)S(1)}, u32[]{:S(2)}, u32[]{:S(2)}) %collective-permute-start.1) | collective-permute-done | bytes 524320 | tf_op jit(solution)/shard_map/ppermute | solution.py:66
  24.3 8.3 %norm_qkv.6 = (f32[128,2048]{1,0:T(8,128)S(1)}, f32[128,512]{1,0:T(8,128)S(1)}, f32[128,128]{1,0:T(8,128)S(1)}) custom-call(s32[2]{0:T(128)S(1)} %pad_add_fusion.2.refs_0_, bf16[128,2048]{1,0:T(8,128)(2,1)S(1)} %slice.41.refs_1_, bf16[128,2048]{1,0:T(8,128)(2,1)S(1)} %collective-permute-done.1.refs_2_, f32[1,8192]{1,0:T(1,128)S(1)} %bitcast.52, ...), custom_call_target="tpu_custom_call" | custom-call | flops 10485760 | bytes 81920 | tf_op jit(solution)/shard_map/norm_qkv/pallas_call | solution.py:244
  39.2 5.5 %collective-permute-done.4.refs_4_ = bf16[128,2048]{1,0:T(8,128)(2,1)S(1)} collective-permute-done((bf16[128,2048]{1,0:T(8,128)(2,1)S(1)}, bf16[128,2048]{1,0:T(8,128)(2,1)S(1)}, u32[]{:S(2)}, u32[]{:S(2)}) %collective-permute-start.4) | collective-permute-done | bytes 524320 | tf_op jit(solution)/shard_map/ppermute | solution.py:75
  54.4 8.6 %norm_qkv.7 = (bf16[128,2048]{1,0:T(8,128)(2,1)S(1)}, bf16[128,512]{1,0:T(8,128)(2,1)S(1)}) custom-call(s32[2]{0:T(128)S(1)} %pad_add_fusion.1.refs_0_, bf16[128,2048]{1,0:T(8,128)(2,1)S(1)} %copy-done.3, bf16[128,2048]{1,0:T(8,128)(2,1)S(1)} %copy-done.25, bf16[128,2048]{1,0:T(8,128)(2,1)S(1)} %copy-done.23, bf16[128,2048]{1,0:T(8,128)(2,1)S(1)} %copy-done.27, ...), custom_call_target="tpu_custom_call" | custom-call | flops 10485760 | bytes 81920 | tf_op jit(solution)/shard_map/norm_qkv/pallas_call | solution.py:244
  63.1 5.6 %prefill_attention.3.refs_1_ = bf16[128,2048]{1,0:T(8,128)(2,1)S(1)} custom-call(s32[4]{0:T(128)S(1)} %copy-done.41, bf16[128,2048]{1,0:T(8,128)(2,1)S(1)} %get-tuple-element.69.q_ref, bf16[1,4,2048,512]{3,2,1,0:T(8,128)(2,1)} %cache_ref.5, bf16[128,512]{1,0:T(8,128)(2,1)S(1)} %get-tuple-element.70.new_ref), custom_call_target="tpu_custom_call" | custom-call | flops 17825792 | bytes 8192 | tf_op jit(solution)/shard_map/prefill_attention/pallas_call | solution.py:453
  76.0 12.3 %project_out.4 = (bf16[128,2048]{1,0:T(8,128)(2,1)S(1)}, bf16[128,2048]{1,0:T(8,128)(2,1)S(1)}, bf16[128,2048]{1,0:T(8,128)(2,1)S(1)}, bf16[128,2048]{1,0:T(8,128)(2,1)S(1)}) custom-call(s32[4]{0:T(128)S(1)} %rev.2.refs_0_, bf16[128,2048]{1,0:T(8,128)(2,1)S(1)} %copy-done.9, bf16[2048,8192]{1,0:T(8,128)(2,1)} %refs_2_.7, ...), custom_call_target="tpu_custom_call" | custom-call | flops 16777216 | bytes 131072 | tf_op jit(solution)/shard_map/project_out/pallas_call | solution.py:323
  89.6 5.2 %collective-permute-done.8.refs_7_.refs_2_ = bf16[256,2048]{1,0:T(8,128)(2,1)S(1)} collective-permute-done((bf16[256,2048]{1,0:T(8,128)(2,1)S(1)}, bf16[256,2048]{1,0:T(8,128)(2,1)S(1)}, u32[]{:S(2)}, u32[]{:S(2)}) %collective-permute-start.8) | collective-permute-done | bytes 1048608 | tf_op jit(solution)/shard_map/ppermute | solution.py:71
  94.8 9.6 %norm_qkv.8 = (f32[256,2048]{1,0:T(8,128)S(1)}, f32[256,512]{1,0:T(8,128)S(1)}, f32[256,128]{1,0:T(8,128)S(1)}) custom-call(s32[2]{0:T(128)S(1)} %pad_add_fusion.2.refs_0_, bf16[256,2048]{1,0:T(8,128)(2,1)S(1)} %copy-done.1, bf16[256,2048]{1,0:T(8,128)(2,1)S(1)} %collective-permute-done.5.refs_3_.refs_2_, f32[1,8192]{1,0:T(1,128)S(1)} %bitcast.54, ...), custom_call_target="tpu_custom_call" | custom-call | flops 20971520 | bytes 81920 | tf_op jit(solution)/shard_map/norm_qkv/pallas_call | solution.py:244
  116.7 13.8 %collective-permute-done.14.refs_4_ = bf16[256,2048]{1,0:T(8,128)(2,1)S(1)} collective-permute-done((bf16[256,2048]{1,0:T(8,128)(2,1)}, bf16[256,2048]{1,0:T(8,128)(2,1)S(1)}, u32[]{:S(2)}, u32[]{:S(2)}) %collective-permute-start.14) | collective-permute-done | bytes 1048608 | tf_op jit(solution)/shard_map/ppermute | solution.py:75
  134.8 12.2 %norm_qkv.9 = (bf16[256,2048]{1,0:T(8,128)(2,1)S(1)}, bf16[256,512]{1,0:T(8,128)(2,1)S(1)}) custom-call(s32[2]{0:T(128)S(1)} %pad_add_fusion.1.refs_0_, bf16[256,2048]{1,0:T(8,128)(2,1)S(1)} %collective-permute-done.6.refs_4_.refs_1_, bf16[256,2048]{1,0:T(8,128)(2,1)S(1)} %collective-permute-done.8.refs_7_.refs_2_, ...), custom_call_target="tpu_custom_call" | custom-call | flops 20971520 | bytes 81920 | tf_op jit(solution)/shard_map/norm_qkv/pallas_call | solution.py:244
  153.8 12.8 %prefill_attention.4.refs_1_ = bf16[256,2048]{1,0:T(8,128)(2,1)S(1)} custom-call(s32[4]{0:T(128)S(1)} %copy-done.41, bf16[256,2048]{1,0:T(8,128)(2,1)S(1)} %get-tuple-element.92.q_ref, bf16[1,4,2048,512]{3,2,1,0:T(8,128)(2,1)} %cache_ref.5, bf16[256,512]{1,0:T(8,128)(2,1)S(1)} %get-tuple-element.93.new_ref), custom_call_target="tpu_custom_call" | custom-call | flops 35651584 | bytes 16384 | tf_op jit(solution)/shard_map/prefill_attention/pallas_call | solution.py:453
  169.7 13.8 %project_out.5 = (bf16[256,2048]{1,0:T(8,128)(2,1)}, bf16[256,2048]{1,0:T(8,128)(2,1)}, bf16[256,2048]{1,0:T(8,128)(2,1)S(1)}, bf16[256,2048]{1,0:T(8,128)(2,1)S(1)}) custom-call(s32[4]{0:T(128)S(1)} %rev.2.refs_0_, bf16[256,2048]{1,0:T(8,128)(2,1)S(1)} %prefill_attention.4.refs_1_, bf16[2048,8192]{1,0:T(8,128)(2,1)} %refs_2_.7, ...), custom_call_target="tpu_custom_call" | custom-call | flops 33554432 | bytes 131072 | tf_op jit(solution)/shard_map/project_out/pallas_call | solution.py:323
  185.8 6.4 %collective-permute-start.20 = (bf16[192,2048]{1,0:T(8,128)(2,1)}, bf16[192,2048]{1,0:T(8,128)(2,1)}, u32[]{:S(2)}, u32[]{:S(2)}) collective-permute-start(bf16[192,2048]{1,0:T(8,128)(2,1)} %collective-permute-done.18.refs_4_.refs_3_), channel_id=1, source_target_pairs={{4,0},{8,12},{5,1},{9,13},{6,2},{10,14},{7,3},{11,15},{20,16},{24,... | collective-permute-start | bytes 2359304 | tf_op jit(solution)/shard_map/ppermute | solution.py:75
  196.0 8.4 %norm_qkv.10 = (f32[192,2048]{1,0:T(8,128)S(1)}, f32[192,512]{1,0:T(8,128)S(1)}, f32[192,128]{1,0:T(8,128)S(1)}) custom-call(s32[2]{0:T(128)S(1)} %pad_add_fusion.2.refs_0_, bf16[192,2048]{1,0:T(8,128)(2,1)S(1)} %pad_maximum_fusion.1.refs_1_, bf16[192,2048]{1,0:T(8,128)(2,1)S(1)} %copy-done.21, f32[1,8192]{1,0:T(1,128)S(1)} %bitcast.56, ...), custom_call_target="tpu_custom_call" | custom-call | flops 15728640 | bytes 81920 | tf_op jit(solution)/shard_map/norm_qkv/pallas_call | solution.py:244
  204.5 14.0 %collective-permute-done.12.refs_14_ = bf16[128,2048]{1,0:T(8,128)(2,1)} collective-permute-done((bf16[128,2048]{1,0:T(8,128)(2,1)}, bf16[128,2048]{1,0:T(8,128)(2,1)}, u32[]{:S(2)}, u32[]{:S(2)}) %collective-permute-start.12) | collective-permute-done | bytes 524320 | tf_op jit(solution)/shard_map/ppermute | solution.py:120
  218.5 11.7 %norm_qkv.11 = (bf16[192,2048]{1,0:T(8,128)(2,1)S(1)}, bf16[192,512]{1,0:T(8,128)(2,1)S(1)}) custom-call(s32[2]{0:T(128)S(1)} %pad_add_fusion.1.refs_0_, bf16[192,2048]{1,0:T(8,128)(2,1)S(1)} %copy-done.19, bf16[192,2048]{1,0:T(8,128)(2,1)S(1)} %collective-permute-done.17.refs_3_.refs_2_, bf16[192,2048]{1,0:T(8,128)(2,1)} %collective-permute-done.18.refs_4_.refs_3_, ...), custom_call_target="tpu_custom_call" | custom-call | flops 15728640 | bytes 81920 | tf_op jit(solution)/shard_map/norm_qkv/pallas_call | solution.py:244
  239.3 5.6 %prefill_attention.5.refs_1_ = bf16[128,2048]{1,0:T(8,128)(2,1)S(1)} custom-call(s32[4]{0:T(128)S(1)} %copy-done.41, bf16[192,2048]{1,0:T(8,128)(2,1)S(1)} %get-tuple-element.107.q_ref, bf16[1,4,2048,512]{3,2,1,0:T(8,128)(2,1)} %cache_ref.5, bf16[128,512]{1,0:T(8,128)(2,1)S(1)} %slice.46.new_ref), custom_call_target="tpu_custom_call" | custom-call | flops 17825792 | bytes 8192 | tf_op jit(solution)/shard_map/prefill_attention/pallas_call | solution.py:453
  244.9 11.1 %collective-permute-done.21 = bf16[256,2048]{1,0:T(8,128)(2,1)} collective-permute-done((bf16[256,2048]{1,0:T(8,128)(2,1)}, bf16[256,2048]{1,0:T(8,128)(2,1)}, u32[]{:S(2)}, u32[]{:S(2)}) %collective-permute-start.21) | collective-permute-done | bytes 1048608 | tf_op jit(solution)/shard_map/ppermute | solution.py:104
  258.7 12.5 %project_out.6 = (bf16[128,2048]{1,0:T(8,128)(2,1)}, bf16[128,2048]{1,0:T(8,128)(2,1)S(1)}, bf16[128,2048]{1,0:T(8,128)(2,1)S(1)}, bf16[128,2048]{1,0:T(8,128)(2,1)S(1)}) custom-call(s32[4]{0:T(128)S(1)} %rev.2.refs_0_, bf16[128,2048]{1,0:T(8,128)(2,1)S(1)} %prefill_attention.5.refs_1_, bf16[2048,8192]{1,0:T(8,128)(2,1)} %refs_2_.7, ...), custom_call_target="tpu_custom_call" | custom-call | flops 16777216 | bytes 131072 | tf_op jit(solution)/shard_map/project_out/pallas_call | solution.py:323
  288.5 7.1 %all-to-all-done = bf16[4,2,128,512]{3,2,1,0:T(8,128)(2,1)} async-done(((bf16[4,2,128,512]{3,2,1,0:T(8,128)(2,1)}), bf16[4,2,128,512]{3,2,1,0:T(8,128)(2,1)}, u32[]{:S(2)}, u32[]{:S(2)}) %all-to-all-start) | async-done | bytes 1048608 | tf_op jit(solution)/shard_map/all_to_all | solution.py:758
  302.7 10.0 %decode_attention.1 = f32[32,2,16,128]{3,2,1,0:T(8,128)S(1)} custom-call(s32[32]{0:T(128)S(1)} %copy-done.42, s32[8]{0:T(128)S(1)} %sub.15.refs_1_, f32[32,2,16,128]{3,2,1,0:T(8,128)S(1)} %bitcast.51, bf16[1,32,64,512]{3,2,1,0:T(8,128)(2,1)S(1)} %copy-done.10, bf16[8,128,512]{2,1,0:T(8,128)(2,1)} %bitcast.17.refs_4_, f32[32,2,512]{2,1,0:T(2,128)S(1)} %bitcast.58, ...), custom_call_target="tpu_custom_call" | custom-call | flops 1048576 | bytes 12288 | tf_op jit(solution)/shard_map/decode_attention/pallas_call | solution.py:565
  316.0 5.8 %collective-permute-done.26 = bf16[128,2048]{1,0:T(8,128)(2,1)} collective-permute-done((bf16[128,2048]{1,0:T(8,128)(2,1)}, bf16[128,2048]{1,0:T(8,128)(2,1)}, u32[]{:S(2)}, u32[]{:S(2)}) %collective-permute-start.26) | collective-permute-done | bytes 524320 | tf_op jit(solution)/shard_map/ppermute | solution.py:104
  328.3 12.3 %project_out.7 = (bf16[64,2048]{1,0:T(8,128)(2,1)S(1)}, bf16[64,2048]{1,0:T(8,128)(2,1)S(1)}, bf16[64,2048]{1,0:T(8,128)(2,1)S(1)}, bf16[64,2048]{1,0:T(8,128)(2,1)S(1)}) custom-call(s32[4]{0:T(128)S(1)} %pad_add_fusion.3.refs_0_, bf16[64,2048]{1,0:T(8,128)(2,1)S(1)} %convert_element_type.239.refs_1_, bf16[2048,8192]{1,0:T(8,128)(2,1)} %refs_2_.7, ...), custom_call_target="tpu_custom_call" | custom-call | flops 8388608 | bytes 131072 | tf_op jit(solution)/shard_map/project_out/pallas_call | solution.py:323
  349.9 13.2 %collective-permute-done.31 = bf16[64,2048]{1,0:T(8,128)(2,1)S(1)} collective-permute-done((bf16[64,2048]{1,0:T(8,128)(2,1)S(1)}, bf16[64,2048]{1,0:T(8,128)(2,1)S(1)}, u32[]{:S(2)}, u32[]{:S(2)}) %collective-permute-start.31) | collective-permute-done | bytes 262176 | tf_op jit(solution)/shard_map/ppermute | solution.py:795
  (213 shorter events, 134.7 us)
Async XLA Ops:
  35.9 33.6 %collective-permute-start.6 = (bf16[256,2048]{1,0:T(8,128)(2,1)S(1)}, bf16[256,2048]{1,0:T(8,128)(2,1)S(1)}, u32[]{:S(2)}, u32[]{:S(2)}) collective-permute-start(bf16[256,2048]{1,0:T(8,128)(2,1)S(1)} %slice.43.refs_1_), channel_id=1, source_target_pairs={{4,8},{8,4},{5,9},{9,5},{6,10},{10,6},{7,11},{11,7},{20,24},{24,20... | collective-permute-start | bytes 3145736 | tf_op jit(solution)/shard_map/ppermute | solution.py:67
  45.5 24.0 %collective-permute-start.5 = (bf16[256,2048]{1,0:T(8,128)(2,1)S(1)}, bf16[256,2048]{1,0:T(8,128)(2,1)S(1)}, u32[]{:S(2)}, u32[]{:S(2)}) collective-permute-start(bf16[256,2048]{1,0:T(8,128)(2,1)S(1)} %slice.43.refs_1_), channel_id=1, source_target_pairs={{0,4},{4,0},{8,12},{12,8},{1,5},{5,1},{9,13},{13,9},{2,6},{6,2},{1... | collective-permute-start | bytes 3145736 | tf_op jit(solution)/shard_map/ppermute | solution.py:66
  69.5 25.3 %collective-permute-start.8 = (bf16[256,2048]{1,0:T(8,128)(2,1)S(1)}, bf16[256,2048]{1,0:T(8,128)(2,1)S(1)}, u32[]{:S(2)}, u32[]{:S(2)}) collective-permute-start(bf16[256,2048]{1,0:T(8,128)(2,1)S(1)} %collective-permute-done.6.refs_4_.refs_1_), channel_id=1, source_target_pairs={{4,0},{8,12},{5,1},{9,13},{6,2},{10,14},{7,3},{11,15},{20,16},{24,... | collective-permute-start | bytes 3145736 | tf_op jit(solution)/shard_map/ppermute | solution.py:71
  72.8 31.7 %collective-permute-start.13 = (bf16[256,2048]{1,0:T(8,128)(2,1)S(1)}, bf16[256,2048]{1,0:T(8,128)(2,1)}, u32[]{:S(2)}, u32[]{:S(2)}) collective-permute-start(bf16[256,2048]{1,0:T(8,128)(2,1)S(1)} %collective-permute-done.5.refs_3_.refs_2_), channel_id=1, source_target_pairs={{4,8},{8,4},{5,9},{9,5},{6,10},{10,6},{7,11},{11,7},{20,24},{24,20... | collective-permute-start | bytes 3145736 | tf_op jit(solution)/shard_map/ppermute | solution.py:72
  88.3 20.8 %collective-permute-start.7 = (bf16[128,2048]{1,0:T(8,128)(2,1)S(1)}, bf16[128,2048]{1,0:T(8,128)(2,1)S(1)}, u32[]{:S(2)}, u32[]{:S(2)}) collective-permute-start(bf16[128,2048]{1,0:T(8,128)(2,1)S(1)} %get-tuple-element.76), channel_id=1, source_target_pairs={{0,4},{12,8},{1,5},{13,9},{2,6},{14,10},{3,7},{15,11},{16,20},{28,... | collective-permute-start | bytes 1572872 | tf_op jit(solution)/shard_map/ppermute | solution.py:99
  104.5 25.9 %collective-permute-start.14 = (bf16[256,2048]{1,0:T(8,128)(2,1)}, bf16[256,2048]{1,0:T(8,128)(2,1)S(1)}, u32[]{:S(2)}, u32[]{:S(2)}) collective-permute-start(bf16[256,2048]{1,0:T(8,128)(2,1)} %collective-permute-done.13.refs_3_), channel_id=1, source_target_pairs={{4,0},{8,12},{5,1},{9,13},{6,2},{10,14},{7,3},{11,15},{20,16},{24,... | collective-permute-start | bytes 3145736 | tf_op jit(solution)/shard_map/ppermute | solution.py:75
  109.2 23.6 %collective-permute-start.9 = (bf16[128,2048]{1,0:T(8,128)(2,1)S(1)}, bf16[128,2048]{1,0:T(8,128)(2,1)S(1)}, u32[]{:S(2)}, u32[]{:S(2)}) collective-permute-start(bf16[128,2048]{1,0:T(8,128)(2,1)S(1)} %get-tuple-element.79), channel_id=1, source_target_pairs={{0,4},{12,8},{1,5},{13,9},{2,6},{14,10},{3,7},{15,11},{16,20},{28,... | collective-permute-start | bytes 1572872 | tf_op jit(solution)/shard_map/ppermute | solution.py:104
  110.7 23.0 %collective-permute-start.10 = (bf16[128,2048]{1,0:T(8,128)(2,1)S(1)}, bf16[128,2048]{1,0:T(8,128)(2,1)S(1)}, u32[]{:S(2)}, u32[]{:S(2)}) collective-permute-start(bf16[128,2048]{1,0:T(8,128)(2,1)S(1)} %add_convert_fusion.11), channel_id=1, source_target_pairs={{4,8},{8,4},{5,9},{9,5},{6,10},{10,6},{7,11},{11,7},{20,24},{24,20... | collective-permute-start | bytes 1572872 | tf_op jit(solution)/shard_map/ppermute | solution.py:105
  112.7 34.3 %collective-permute-start.16 = (bf16[192,2048]{1,0:T(8,128)(2,1)S(1)}, bf16[192,2048]{1,0:T(8,128)(2,1)S(1)}, u32[]{:S(2)}, u32[]{:S(2)}) collective-permute-start(bf16[192,2048]{1,0:T(8,128)(2,1)S(1)} %pad_maximum_fusion.1.refs_1_), channel_id=1, source_target_pairs={{4,8},{8,4},{5,9},{9,5},{6,10},{10,6},{7,11},{11,7},{20,24},{24,20... | collective-permute-start | bytes 2359304 | tf_op jit(solution)/shard_map/ppermute | solution.py:67
  148.2 18.4 %collective-permute-start.17 = (bf16[192,2048]{1,0:T(8,128)(2,1)S(1)}, bf16[192,2048]{1,0:T(8,128)(2,1)S(1)}, u32[]{:S(2)}, u32[]{:S(2)}) collective-permute-start(bf16[192,2048]{1,0:T(8,128)(2,1)S(1)} %collective-permute-done.16.refs_1_), channel_id=1, source_target_pairs={{4,0},{8,12},{5,1},{9,13},{6,2},{10,14},{7,3},{11,15},{20,16},{24,... | collective-permute-start | bytes 2359304 | tf_op jit(solution)/shard_map/ppermute | solution.py:71
  184.5 46.4 %collective-permute-start.19 = (bf16[256,2048]{1,0:T(8,128)(2,1)}, bf16[256,2048]{1,0:T(8,128)(2,1)}, u32[]{:S(2)}, u32[]{:S(2)}) collective-permute-start(bf16[256,2048]{1,0:T(8,128)(2,1)} %get-tuple-element.98), channel_id=1, source_target_pairs={{0,4},{12,8},{1,5},{13,9},{2,6},{14,10},{3,7},{15,11},{16,20},{28,... | collective-permute-start | bytes 3145736 | tf_op jit(solution)/shard_map/ppermute | solution.py:99
  185.8 32.7 %collective-permute-start.20 = (bf16[192,2048]{1,0:T(8,128)(2,1)}, bf16[192,2048]{1,0:T(8,128)(2,1)}, u32[]{:S(2)}, u32[]{:S(2)}) collective-permute-start(bf16[192,2048]{1,0:T(8,128)(2,1)} %collective-permute-done.18.refs_4_.refs_3_), channel_id=1, source_target_pairs={{4,0},{8,12},{5,1},{9,13},{6,2},{10,14},{7,3},{11,15},{20,16},{24,... | collective-permute-start | bytes 2359304 | tf_op jit(solution)/shard_map/ppermute | solution.py:75
  194.6 23.9 %collective-permute-start.12 = (bf16[128,2048]{1,0:T(8,128)(2,1)}, bf16[128,2048]{1,0:T(8,128)(2,1)}, u32[]{:S(2)}, u32[]{:S(2)}) collective-permute-start(bf16[128,2048]{1,0:T(8,128)(2,1)} %add_convert_fusion.9.refs_14_), channel_id=1, source_target_pairs={{0,4},{4,0},{8,12},{12,8},{1,5},{5,1},{9,13},{13,9},{2,6},{6,2},{1... | collective-permute-start | bytes 1572872 | tf_op jit(solution)/shard_map/ppermute | solution.py:120
  234.2 21.8 %collective-permute-start.21 = (bf16[256,2048]{1,0:T(8,128)(2,1)}, bf16[256,2048]{1,0:T(8,128)(2,1)}, u32[]{:S(2)}, u32[]{:S(2)}) collective-permute-start(bf16[256,2048]{1,0:T(8,128)(2,1)} %get-tuple-element.104), channel_id=1, source_target_pairs={{0,4},{12,8},{1,5},{13,9},{2,6},{14,10},{3,7},{15,11},{16,20},{28,... | collective-permute-start | bytes 3145736 | tf_op jit(solution)/shard_map/ppermute | solution.py:104
  235.9 22.4 %collective-permute-start.22 = (bf16[256,2048]{1,0:T(8,128)(2,1)}, bf16[256,2048]{1,0:T(8,128)(2,1)S(1)}, u32[]{:S(2)}, u32[]{:S(2)}) collective-permute-start(bf16[256,2048]{1,0:T(8,128)(2,1)} %add_convert_fusion.3), channel_id=1, source_target_pairs={{4,8},{8,4},{5,9},{9,5},{6,10},{10,6},{7,11},{11,7},{20,24},{24,20... | collective-permute-start | bytes 3145736 | tf_op jit(solution)/shard_map/ppermute | solution.py:105
  276.7 18.8 %all-to-all-start = ((bf16[4,2,128,512]{3,2,1,0:T(8,128)(2,1)}), bf16[4,2,128,512]{3,2,1,0:T(8,128)(2,1)}, u32[]{:S(2)}, u32[]{:S(2)}) async-start(bf16[4,2,128,512]{3,2,1,0:T(8,128)(2,1)} %copy.35), calls=%async_computation | async-start | bytes 2097152 | tf_op jit(solution)/shard_map/all_to_all | solution.py:758
  281.2 33.3 %collective-permute-start.23 = (bf16[256,2048]{1,0:T(8,128)(2,1)S(1)}, bf16[256,2048]{1,0:T(8,128)(2,1)}, u32[]{:S(2)}, u32[]{:S(2)}) collective-permute-start(bf16[256,2048]{1,0:T(8,128)(2,1)S(1)} %add_convert_fusion.2.refs_3_), channel_id=1, source_target_pairs={{4,8},{8,4},{5,9},{9,5},{6,10},{10,6},{7,11},{11,7},{20,24},{24,20... | collective-permute-start | bytes 3145736 | tf_op jit(solution)/shard_map/ppermute | solution.py:119
  285.1 30.1 %collective-permute-start.24 = (bf16[256,2048]{1,0:T(8,128)(2,1)S(1)}, bf16[256,2048]{1,0:T(8,128)(2,1)}, u32[]{:S(2)}, u32[]{:S(2)}) collective-permute-start(bf16[256,2048]{1,0:T(8,128)(2,1)S(1)} %add_convert_fusion.1.refs_4_), channel_id=1, source_target_pairs={{0,4},{4,0},{8,12},{12,8},{1,5},{5,1},{9,13},{13,9},{2,6},{6,2},{1... | collective-permute-start | bytes 3145736 | tf_op jit(solution)/shard_map/ppermute | solution.py:120
  295.5 26.3 %collective-permute-start.26 = (bf16[128,2048]{1,0:T(8,128)(2,1)}, bf16[128,2048]{1,0:T(8,128)(2,1)}, u32[]{:S(2)}, u32[]{:S(2)}) collective-permute-start(bf16[128,2048]{1,0:T(8,128)(2,1)} %copy-done.33), channel_id=1, source_target_pairs={{0,4},{12,8},{1,5},{13,9},{2,6},{14,10},{3,7},{15,11},{16,20},{28,... | collective-permute-start | bytes 1572872 | tf_op jit(solution)/shard_map/ppermute | solution.py:104
  298.7 24.4 %collective-permute-start.27 = (bf16[128,2048]{1,0:T(8,128)(2,1)}, bf16[128,2048]{1,0:T(8,128)(2,1)}, u32[]{:S(2)}, u32[]{:S(2)}) collective-permute-start(bf16[128,2048]{1,0:T(8,128)(2,1)} %add_convert_fusion.7.refs_6_), channel_id=1, source_target_pairs={{4,8},{8,4},{5,9},{9,5},{6,10},{10,6},{7,11},{11,7},{20,24},{24,20... | collective-permute-start | bytes 1572872 | tf_op jit(solution)/shard_map/ppermute | solution.py:105
  324.6 43.0 %collective-permute-start.28 = (bf16[128,2048]{1,0:T(8,128)(2,1)S(1)}, bf16[128,2048]{1,0:T(8,128)(2,1)S(1)}, u32[]{:S(2)}, u32[]{:S(2)}) collective-permute-start(bf16[128,2048]{1,0:T(8,128)(2,1)S(1)} %add_convert_fusion.6.refs_3_), channel_id=1, source_target_pairs={{4,8},{8,4},{5,9},{9,5},{6,10},{10,6},{7,11},{11,7},{20,24},{24,20... | collective-permute-start | bytes 1572872 | tf_op jit(solution)/shard_map/ppermute | solution.py:119
  328.3 39.3 %collective-permute-start.29 = (bf16[128,2048]{1,0:T(8,128)(2,1)S(1)}, bf16[128,2048]{1,0:T(8,128)(2,1)S(1)}, u32[]{:S(2)}, u32[]{:S(2)}) collective-permute-start(bf16[128,2048]{1,0:T(8,128)(2,1)S(1)} %add_convert_fusion.5.refs_4_), channel_id=1, source_target_pairs={{0,4},{4,0},{8,12},{12,8},{1,5},{5,1},{9,13},{13,9},{2,6},{6,2},{1... | collective-permute-start | bytes 1572872 | tf_op jit(solution)/shard_map/ppermute | solution.py:120
  341.1 22.1 %collective-permute-start.31 = (bf16[64,2048]{1,0:T(8,128)(2,1)S(1)}, bf16[64,2048]{1,0:T(8,128)(2,1)S(1)}, u32[]{:S(2)}, u32[]{:S(2)}) collective-permute-start(bf16[64,2048]{1,0:T(8,128)(2,1)S(1)} %get-tuple-element.122), channel_id=1, source_target_pairs={{0,8},{4,12},{8,0},{12,4},{1,9},{5,13},{9,1},{13,5},{2,10},{6,14},... | collective-permute-start | bytes 786440 | tf_op jit(solution)/shard_map/ppermute | solution.py:795
  345.1 21.6 %collective-permute-start.32 = (bf16[64,2048]{1,0:T(8,128)(2,1)S(1)}, bf16[64,2048]{1,0:T(8,128)(2,1)S(1)}, u32[]{:S(2)}, u32[]{:S(2)}) collective-permute-start(bf16[64,2048]{1,0:T(8,128)(2,1)S(1)} %get-tuple-element.123), channel_id=1, source_target_pairs={{0,12},{4,0},{8,4},{12,8},{1,13},{5,1},{9,5},{13,9},{2,14},{6,2},{... | collective-permute-start | bytes 786440 | tf_op jit(solution)/shard_map/ppermute | solution.py:795
  (62 other events, 677.0 us)

commit v2 on v1

--- a/solution.py
+++ b/solution.py
@@ -672,14 +672,11 @@
     if on_line:
         first = LineGather(blocks[0], "tensor")
         first.second()
-        begun = project_part(
-            [[first.block], [first.partner]], order[:2], *weights, None, None, (first.middle,)
-        )
-        first.third(begun[2])
+        first.third()
         second = LineGather(
-            blocks[1], "tensor", (first.outer_far,), (first.outer, first.middle_far, begun[2])
-        )
-        queries, new_kv = project_part(first.slots()[2:], order[2:], *weights, begun, scales)
+            blocks[1], "tensor", (first.outer_far,), (first.outer, first.middle_far)
+        )
+        queries, new_kv = project_part(first.slots(), order, *weights, None, scales)
         keep(new_kv)
         attended = attention(0, queries)
         second.second(attended)
@@ -783,14 +780,14 @@
     )
     if on_line:
         to = [(tensor_index + shift) % tensor_count for shift in range(tensor_count)]
-        sums[2].third(dec_attended)
         own, *parts = project_out(
             dec_attended,
             w_o,
             jnp.stack(to).astype(jnp.int32),
             block_width,
-            held=(*sums[2].second_hop, *corners(sums[1].terms[1:])),
-        )
+            held=corners(sums[1].terms[1:]),
+        )
+        sums[2].third(own)
         dec_terms = [own] + [
             lax.ppermute(
                 part, "tensor", [(j, (j + shift) % tensor_count) for j in range(tensor_count)]

time: 377 us -> 390 us (1.034)
  the two profiles are of different devices: /device:TPU:12 before, /device:TPU:10 now
where the time goes in v2:
time: 390 us; the launch traced here: 384 us
  Pallas kernels  150 us (38%)
  starting transfers between devices  108 us (28%)
  waiting for transfers between devices  79.7 us (20%)
  local copies, waits for them, and re-layouts  23.2 us (6%)
  other arithmetic  20.4 us (5%)
    pallas_call x5, Pallas kernels, project_part(): pl.pallas_call(without(kernel, 1 + len(operands), len(held)), grid_spec=p...  56.3 us
    pallas_call x4, Pallas kernels, project_out(): pl.pallas_call(without(functools.partial(out_kernel, count, stacked, tile...  50.9 us
    all_to_all x1, starting transfers between devices, shards(): lax.all_to_all(outgoing, 'section', split_axis=0, concat_axis=0, tiled=True)  31.1 us
    pallas_call x3, Pallas kernels, prefill_attention(): pl.pallas_call(functools.partial(prefill_kernel, kv_heads, group, span, f...  30 us
    ppermute x3, waiting for transfers between devices, third(): lax.ppermute(after(self.middle_far, *held), self.axis, OUTWARD)  18.5 us
    unnamed x95, local copies, waits for them, and re-layouts  16.1 us
    ppermute x3, waiting for transfers between devices, shards(): lax.ppermute(part, 'tensor', [(j, (j + shift) % tensor_count) for j in ra...  14.2 us
    pallas_call x1, Pallas kernels, decode_attention(): pl.pallas_call(without(functools.partial(decode_kernel, kv_heads, batch),...  12.8 us
  transfers between devices with their start and end apart: 34, of which 11 were waited for; matrix products, arithmetic and copies ran while one was open for 6% of the time, Pallas kernels for 32%

profile of v2, /device:TPU:10, one launch (start us, length us, event | category | flops | bytes accessed | tf_op | source)
XLA Modules:
  0.0 383.7 jit_solution(10605927919743775094)
XLA Ops:
  6.2 11.2 %collective-permute-done.1.refs_3_ = bf16[128,2048]{1,0:T(8,128)(2,1)S(1)} collective-permute-done((bf16[128,2048]{1,0:T(8,128)(2,1)S(1)}, bf16[128,2048]{1,0:T(8,128)(2,1)S(1)}, u32[]{:S(2)}, u32[]{:S(2)}) %collective-permute-start.1) | collective-permute-done | bytes 524320 | tf_op jit(solution)/shard_map/ppermute | solution.py:67
  23.3 9.9 %collective-permute-done.3.refs_5_ = bf16[128,2048]{1,0:T(8,128)(2,1)S(1)} collective-permute-done((bf16[128,2048]{1,0:T(8,128)(2,1)S(1)}, bf16[128,2048]{1,0:T(8,128)(2,1)S(1)}, u32[]{:S(2)}, u32[]{:S(2)}) %collective-permute-start.3) | collective-permute-done | bytes 524320 | tf_op jit(solution)/shard_map/ppermute | solution.py:72
  39.5 5.0 %collective-permute-done.4.refs_6_ = bf16[128,2048]{1,0:T(8,128)(2,1)S(1)} collective-permute-done((bf16[128,2048]{1,0:T(8,128)(2,1)S(1)}, bf16[128,2048]{1,0:T(8,128)(2,1)S(1)}, u32[]{:S(2)}, u32[]{:S(2)}) %collective-permute-start.4) | collective-permute-done | bytes 524320 | tf_op jit(solution)/shard_map/ppermute | solution.py:75
  54.2 14.6 %norm_qkv.5 = (bf16[128,2048]{1,0:T(8,128)(2,1)S(1)}, bf16[128,512]{1,0:T(8,128)(2,1)S(1)}) custom-call(s32[4]{0:T(128)S(1)} %pad_add_fusion.refs_0_, bf16[128,2048]{1,0:T(8,128)(2,1)S(1)} %copy-done.9, bf16[128,2048]{1,0:T(8,128)(2,1)S(1)} %copy-done.22, bf16[128,2048]{1,0:T(8,128)(2,1)S(1)} %copy-done.20, bf16[128,2048]{1,0:T(8,128)(2,1)S(1)} %copy-done.26, ...), custom_call_target="tpu_custom_call" | custom-call | flops 20971520 | bytes 163840 | tf_op jit(solution)/shard_map/norm_qkv/pallas_call | solution.py:244
  68.8 8.6 %prefill_attention.3.refs_1_ = bf16[128,2048]{1,0:T(8,128)(2,1)S(1)} custom-call(s32[4]{0:T(128)S(1)} %copy-done.38, bf16[128,2048]{1,0:T(8,128)(2,1)S(1)} %get-tuple-element.61.q_ref, bf16[1,4,2048,512]{3,2,1,0:T(8,128)(2,1)} %cache_ref.5, bf16[128,512]{1,0:T(8,128)(2,1)S(1)} %get-tuple-element.62.new_ref), custom_call_target="tpu_custom_call" | custom-call | flops 17825792 | bytes 8192 | tf_op jit(solution)/shard_map/prefill_attention/pallas_call | solution.py:453
  84.8 12.3 %project_out.4 = (bf16[128,2048]{1,0:T(8,128)(2,1)S(1)}, bf16[128,2048]{1,0:T(8,128)(2,1)S(1)}, bf16[128,2048]{1,0:T(8,128)(2,1)S(1)}, bf16[128,2048]{1,0:T(8,128)(2,1)S(1)}) custom-call(s32[4]{0:T(128)S(1)} %rev.2.refs_0_, bf16[128,2048]{1,0:T(8,128)(2,1)S(1)} %copy-done.7, bf16[2048,8192]{1,0:T(8,128)(2,1)} %refs_2_.7, ...), custom_call_target="tpu_custom_call" | custom-call | flops 16777216 | bytes 131072 | tf_op jit(solution)/shard_map/project_out/pallas_call | solution.py:323
  98.5 9.3 %norm_qkv.6 = (f32[256,2048]{1,0:T(8,128)S(1)}, f32[256,512]{1,0:T(8,128)S(1)}, f32[256,128]{1,0:T(8,128)S(1)}) custom-call(s32[2]{0:T(128)S(1)} %pad_add_fusion.1.refs_0_, bf16[256,2048]{1,0:T(8,128)(2,1)S(1)} %copy-done.1, bf16[256,2048]{1,0:T(8,128)(2,1)S(1)} %collective-permute-done.5.refs_3_.refs_2_, f32[1,8192]{1,0:T(1,128)S(1)} %bitcast.53, ...), custom_call_target="tpu_custom_call" | custom-call | flops 20971520 | bytes 81920 | tf_op jit(solution)/shard_map/norm_qkv/pallas_call | solution.py:244
  107.8 4.8 %collective-permute-start.14 = (bf16[256,2048]{1,0:T(8,128)(2,1)}, bf16[256,2048]{1,0:T(8,128)(2,1)S(1)}, u32[]{:S(2)}, u32[]{:S(2)}) collective-permute-start(bf16[256,2048]{1,0:T(8,128)(2,1)} %collective-permute-done.13.refs_3_), channel_id=1, source_target_pairs={{4,0},{8,12},{5,1},{9,13},{6,2},{10,14},{7,3},{11,15},{20,16},{24,... | collective-permute-start | bytes 3145736 | tf_op jit(solution)/shard_map/ppermute | solution.py:75
  120.3 13.5 %collective-permute-done.14.refs_4_ = bf16[256,2048]{1,0:T(8,128)(2,1)S(1)} collective-permute-done((bf16[256,2048]{1,0:T(8,128)(2,1)}, bf16[256,2048]{1,0:T(8,128)(2,1)S(1)}, u32[]{:S(2)}, u32[]{:S(2)}) %collective-permute-start.14) | collective-permute-done | bytes 1048608 | tf_op jit(solution)/shard_map/ppermute | solution.py:75
  138.0 12.2 %norm_qkv.7 = (bf16[256,2048]{1,0:T(8,128)(2,1)S(1)}, bf16[256,512]{1,0:T(8,128)(2,1)S(1)}) custom-call(s32[2]{0:T(128)S(1)} %pad_add_fusion.2.refs_0_, bf16[256,2048]{1,0:T(8,128)(2,1)S(1)} %collective-permute-done.6.refs_4_.refs_1_, bf16[256,2048]{1,0:T(8,128)(2,1)S(1)} %collective-permute-done.8.refs_7_.refs_2_, ...), custom_call_target="tpu_custom_call" | custom-call | flops 20971520 | bytes 81920 | tf_op jit(solution)/shard_map/norm_qkv/pallas_call | solution.py:244
  156.8 14.3 %prefill_attention.4.refs_1_ = bf16[256,2048]{1,0:T(8,128)(2,1)S(1)} custom-call(s32[4]{0:T(128)S(1)} %copy-done.38, bf16[256,2048]{1,0:T(8,128)(2,1)S(1)} %get-tuple-element.84.q_ref, bf16[1,4,2048,512]{3,2,1,0:T(8,128)(2,1)} %cache_ref.5, bf16[256,512]{1,0:T(8,128)(2,1)S(1)} %get-tuple-element.85.new_ref), custom_call_target="tpu_custom_call" | custom-call | flops 35651584 | bytes 16384 | tf_op jit(solution)/shard_map/prefill_attention/pallas_call | solution.py:453
  171.2 13.8 %project_out.5 = (bf16[256,2048]{1,0:T(8,128)(2,1)}, bf16[256,2048]{1,0:T(8,128)(2,1)}, bf16[256,2048]{1,0:T(8,128)(2,1)S(1)}, bf16[256,2048]{1,0:T(8,128)(2,1)S(1)}) custom-call(s32[4]{0:T(128)S(1)} %rev.2.refs_0_, bf16[256,2048]{1,0:T(8,128)(2,1)S(1)} %prefill_attention.4.refs_1_, bf16[2048,8192]{1,0:T(8,128)(2,1)} %refs_2_.7, ...), custom_call_target="tpu_custom_call" | custom-call | flops 33554432 | bytes 131072 | tf_op jit(solution)/shard_map/project_out/pallas_call | solution.py:323
  187.3 6.4 %collective-permute-start.20 = (bf16[192,2048]{1,0:T(8,128)(2,1)}, bf16[192,2048]{1,0:T(8,128)(2,1)}, u32[]{:S(2)}, u32[]{:S(2)}) collective-permute-start(bf16[192,2048]{1,0:T(8,128)(2,1)} %collective-permute-done.18.refs_4_.refs_3_), channel_id=1, source_target_pairs={{4,0},{8,12},{5,1},{9,13},{6,2},{10,14},{7,3},{11,15},{20,16},{24,... | collective-permute-start | bytes 2359304 | tf_op jit(solution)/shard_map/ppermute | solution.py:75
  198.2 8.4 %norm_qkv.8 = (f32[192,2048]{1,0:T(8,128)S(1)}, f32[192,512]{1,0:T(8,128)S(1)}, f32[192,128]{1,0:T(8,128)S(1)}) custom-call(s32[2]{0:T(128)S(1)} %pad_add_fusion.1.refs_0_, bf16[192,2048]{1,0:T(8,128)(2,1)S(1)} %pad_maximum_fusion.1.refs_1_, bf16[192,2048]{1,0:T(8,128)(2,1)S(1)} %copy-done.18, f32[1,8192]{1,0:T(1,128)S(1)} %bitcast.55, ...), custom_call_target="tpu_custom_call" | custom-call | flops 15728640 | bytes 81920 | tf_op jit(solution)/shard_map/norm_qkv/pallas_call | solution.py:244
  211.3 11.7 %norm_qkv.9 = (bf16[192,2048]{1,0:T(8,128)(2,1)S(1)}, bf16[192,512]{1,0:T(8,128)(2,1)S(1)}) custom-call(s32[2]{0:T(128)S(1)} %pad_add_fusion.2.refs_0_, bf16[192,2048]{1,0:T(8,128)(2,1)S(1)} %copy-done.16, bf16[192,2048]{1,0:T(8,128)(2,1)S(1)} %collective-permute-done.17.refs_3_.refs_2_, bf16[192,2048]{1,0:T(8,128)(2,1)} %collective-permute-done.18.refs_4_.refs_3_, ...), custom_call_target="tpu_custom_call" | custom-call | flops 15728640 | bytes 81920 | tf_op jit(solution)/shard_map/norm_qkv/pallas_call | solution.py:244
  230.2 7.1 %prefill_attention.5.refs_1_ = bf16[128,2048]{1,0:T(8,128)(2,1)S(1)} custom-call(s32[4]{0:T(128)S(1)} %copy-done.38, bf16[192,2048]{1,0:T(8,128)(2,1)S(1)} %get-tuple-element.99.q_ref, bf16[1,4,2048,512]{3,2,1,0:T(8,128)(2,1)} %cache_ref.5, bf16[128,512]{1,0:T(8,128)(2,1)S(1)} %slice.44.new_ref), custom_call_target="tpu_custom_call" | custom-call | flops 17825792 | bytes 8192 | tf_op jit(solution)/shard_map/prefill_attention/pallas_call | solution.py:453
  237.3 5.0 %collective-permute-done.21 = bf16[256,2048]{1,0:T(8,128)(2,1)} collective-permute-done((bf16[256,2048]{1,0:T(8,128)(2,1)}, bf16[256,2048]{1,0:T(8,128)(2,1)}, u32[]{:S(2)}, u32[]{:S(2)}) %collective-permute-start.21) | collective-permute-done | bytes 1048608 | tf_op jit(solution)/shard_map/ppermute | solution.py:104
  244.7 12.5 %project_out.6 = (bf16[128,2048]{1,0:T(8,128)(2,1)}, bf16[128,2048]{1,0:T(8,128)(2,1)S(1)}, bf16[128,2048]{1,0:T(8,128)(2,1)S(1)}, bf16[128,2048]{1,0:T(8,128)(2,1)S(1)}) custom-call(s32[4]{0:T(128)S(1)} %rev.2.refs_0_, bf16[128,2048]{1,0:T(8,128)(2,1)S(1)} %prefill_attention.5.refs_1_, bf16[2048,8192]{1,0:T(8,128)(2,1)} %refs_2_.7, ...), custom_call_target="tpu_custom_call" | custom-call | flops 16777216 | bytes 131072 | tf_op jit(solution)/shard_map/project_out/pallas_call | solution.py:323
  262.7 31.1 %all-to-all-start = ((bf16[4,2,128,512]{3,2,1,0:T(8,128)(2,1)}), bf16[4,2,128,512]{3,2,1,0:T(8,128)(2,1)}, u32[]{:S(2)}, u32[]{:S(2)}) async-start(bf16[4,2,128,512]{3,2,1,0:T(8,128)(2,1)} %copy.35), calls=%async_computation | async-start | bytes 2097152 | tf_op jit(solution)/shard_map/all_to_all | solution.py:755
  301.3 5.4 %all-to-all-done = bf16[4,2,128,512]{3,2,1,0:T(8,128)(2,1)} async-done(((bf16[4,2,128,512]{3,2,1,0:T(8,128)(2,1)}), bf16[4,2,128,512]{3,2,1,0:T(8,128)(2,1)}, u32[]{:S(2)}, u32[]{:S(2)}) %all-to-all-start) | async-done | bytes 1048608 | tf_op jit(solution)/shard_map/all_to_all | solution.py:755
  313.4 12.8 %decode_attention.1 = f32[32,2,16,128]{3,2,1,0:T(8,128)S(1)} custom-call(s32[32]{0:T(128)S(1)} %copy-done.39, s32[8]{0:T(128)S(1)} %sub.15.refs_1_, f32[32,2,16,128]{3,2,1,0:T(8,128)S(1)} %bitcast.51, bf16[1,32,64,512]{3,2,1,0:T(8,128)(2,1)S(1)} %copy-done.10, bf16[8,128,512]{2,1,0:T(8,128)(2,1)} %bitcast.21.refs_4_, f32[32,2,512]{2,1,0:T(2,128)S(1)} %bitcast.57, ...), custom_call_target="tpu_custom_call" | custom-call | flops 1048576 | bytes 12288 | tf_op jit(solution)/shard_map/decode_attention/pallas_call | solution.py:565
  329.5 12.3 %project_out.7 = (bf16[64,2048]{1,0:T(8,128)(2,1)S(1)}, bf16[64,2048]{1,0:T(8,128)(2,1)S(1)}, bf16[64,2048]{1,0:T(8,128)(2,1)S(1)}, bf16[64,2048]{1,0:T(8,128)(2,1)S(1)}) custom-call(s32[4]{0:T(128)S(1)} %pad_add_fusion.3.refs_0_, bf16[64,2048]{1,0:T(8,128)(2,1)S(1)} %convert_element_type.239.refs_1_, bf16[2048,8192]{1,0:T(8,128)(2,1)} %refs_2_.7, ...), custom_call_target="tpu_custom_call" | custom-call | flops 8388608 | bytes 131072 | tf_op jit(solution)/shard_map/project_out/pallas_call | solution.py:323
  355.4 10.6 %collective-permute-done.31 = bf16[64,2048]{1,0:T(8,128)(2,1)S(1)} collective-permute-done((bf16[64,2048]{1,0:T(8,128)(2,1)S(1)}, bf16[64,2048]{1,0:T(8,128)(2,1)S(1)}, u32[]{:S(2)}, u32[]{:S(2)}) %collective-permute-start.31) | collective-permute-done | bytes 262176 | tf_op jit(solution)/shard_map/ppermute | solution.py:792
  370.5 9.4 %collective-permute-done.28 = bf16[128,2048]{1,0:T(8,128)(2,1)S(1)} collective-permute-done((bf16[128,2048]{1,0:T(8,128)(2,1)S(1)}, bf16[128,2048]{1,0:T(8,128)(2,1)S(1)}, u32[]{:S(2)}, u32[]{:S(2)}) %collective-permute-start.28) | collective-permute-done | bytes 524320 | tf_op jit(solution)/shard_map/ppermute | solution.py:119
  (204 shorter events, 119.2 us)
Async XLA Ops:
  37.1 41.1 %collective-permute-start.6 = (bf16[256,2048]{1,0:T(8,128)(2,1)S(1)}, bf16[256,2048]{1,0:T(8,128)(2,1)S(1)}, u32[]{:S(2)}, u32[]{:S(2)}) collective-permute-start(bf16[256,2048]{1,0:T(8,128)(2,1)S(1)} %slice.41.refs_1_), channel_id=1, source_target_pairs={{4,8},{8,4},{5,9},{9,5},{6,10},{10,6},{7,11},{11,7},{20,24},{24,20... | collective-permute-start | bytes 3145736 | tf_op jit(solution)/shard_map/ppermute | solution.py:67
  45.3 32.9 %collective-permute-start.5 = (bf16[256,2048]{1,0:T(8,128)(2,1)S(1)}, bf16[256,2048]{1,0:T(8,128)(2,1)S(1)}, u32[]{:S(2)}, u32[]{:S(2)}) collective-permute-start(bf16[256,2048]{1,0:T(8,128)(2,1)S(1)} %slice.41.refs_1_), channel_id=1, source_target_pairs={{0,4},{4,0},{8,12},{12,8},{1,5},{5,1},{9,13},{13,9},{2,6},{6,2},{1... | collective-permute-start | bytes 3145736 | tf_op jit(solution)/shard_map/ppermute | solution.py:66
  78.2 20.2 %collective-permute-start.8 = (bf16[256,2048]{1,0:T(8,128)(2,1)S(1)}, bf16[256,2048]{1,0:T(8,128)(2,1)S(1)}, u32[]{:S(2)}, u32[]{:S(2)}) collective-permute-start(bf16[256,2048]{1,0:T(8,128)(2,1)S(1)} %collective-permute-done.6.refs_4_.refs_1_), channel_id=1, source_target_pairs={{4,0},{8,12},{5,1},{9,13},{6,2},{10,14},{7,3},{11,15},{20,16},{24,... | collective-permute-start | bytes 3145736 | tf_op jit(solution)/shard_map/ppermute | solution.py:71
  80.2 27.6 %collective-permute-start.13 = (bf16[256,2048]{1,0:T(8,128)(2,1)S(1)}, bf16[256,2048]{1,0:T(8,128)(2,1)}, u32[]{:S(2)}, u32[]{:S(2)}) collective-permute-start(bf16[256,2048]{1,0:T(8,128)(2,1)S(1)} %collective-permute-done.5.refs_3_.refs_2_), channel_id=1, source_target_pairs={{4,8},{8,4},{5,9},{9,5},{6,10},{10,6},{7,11},{11,7},{20,24},{24,20... | collective-permute-start | bytes 3145736 | tf_op jit(solution)/shard_map/ppermute | solution.py:72
  107.8 25.9 %collective-permute-start.14 = (bf16[256,2048]{1,0:T(8,128)(2,1)}, bf16[256,2048]{1,0:T(8,128)(2,1)S(1)}, u32[]{:S(2)}, u32[]{:S(2)}) collective-permute-start(bf16[256,2048]{1,0:T(8,128)(2,1)} %collective-permute-done.13.refs_3_), channel_id=1, source_target_pairs={{4,0},{8,12},{5,1},{9,13},{6,2},{10,14},{7,3},{11,15},{20,16},{24,... | collective-permute-start | bytes 3145736 | tf_op jit(solution)/shard_map/ppermute | solution.py:75
  112.8 23.3 %collective-permute-start.9 = (bf16[128,2048]{1,0:T(8,128)(2,1)S(1)}, bf16[128,2048]{1,0:T(8,128)(2,1)S(1)}, u32[]{:S(2)}, u32[]{:S(2)}) collective-permute-start(bf16[128,2048]{1,0:T(8,128)(2,1)S(1)} %get-tuple-element.71), channel_id=1, source_target_pairs={{0,4},{12,8},{1,5},{13,9},{2,6},{14,10},{3,7},{15,11},{16,20},{28,... | collective-permute-start | bytes 1572872 | tf_op jit(solution)/shard_map/ppermute | solution.py:104
  114.2 22.9 %collective-permute-start.10 = (bf16[128,2048]{1,0:T(8,128)(2,1)S(1)}, bf16[128,2048]{1,0:T(8,128)(2,1)S(1)}, u32[]{:S(2)}, u32[]{:S(2)}) collective-permute-start(bf16[128,2048]{1,0:T(8,128)(2,1)S(1)} %add_convert_fusion.11), channel_id=1, source_target_pairs={{4,8},{8,4},{5,9},{9,5},{6,10},{10,6},{7,11},{11,7},{20,24},{24,20... | collective-permute-start | bytes 1572872 | tf_op jit(solution)/shard_map/ppermute | solution.py:105
  117.4 32.9 %collective-permute-start.16 = (bf16[192,2048]{1,0:T(8,128)(2,1)S(1)}, bf16[192,2048]{1,0:T(8,128)(2,1)S(1)}, u32[]{:S(2)}, u32[]{:S(2)}) collective-permute-start(bf16[192,2048]{1,0:T(8,128)(2,1)S(1)} %pad_maximum_fusion.1.refs_1_), channel_id=1, source_target_pairs={{4,8},{8,4},{5,9},{9,5},{6,10},{10,6},{7,11},{11,7},{20,24},{24,20... | collective-permute-start | bytes 2359304 | tf_op jit(solution)/shard_map/ppermute | solution.py:67
  150.3 20.9 %collective-permute-start.17 = (bf16[192,2048]{1,0:T(8,128)(2,1)S(1)}, bf16[192,2048]{1,0:T(8,128)(2,1)S(1)}, u32[]{:S(2)}, u32[]{:S(2)}) collective-permute-start(bf16[192,2048]{1,0:T(8,128)(2,1)S(1)} %collective-permute-done.16.refs_1_), channel_id=1, source_target_pairs={{4,0},{8,12},{5,1},{9,13},{6,2},{10,14},{7,3},{11,15},{20,16},{24,... | collective-permute-start | bytes 2359304 | tf_op jit(solution)/shard_map/ppermute | solution.py:71
  153.9 17.3 %collective-permute-start.18 = (bf16[192,2048]{1,0:T(8,128)(2,1)S(1)}, bf16[192,2048]{1,0:T(8,128)(2,1)}, u32[]{:S(2)}, u32[]{:S(2)}) collective-permute-start(bf16[192,2048]{1,0:T(8,128)(2,1)S(1)} %collective-permute-done.15.refs_2_), channel_id=1, source_target_pairs={{4,8},{8,4},{5,9},{9,5},{6,10},{10,6},{7,11},{11,7},{20,24},{24,20... | collective-permute-start | bytes 2359304 | tf_op jit(solution)/shard_map/ppermute | solution.py:72
  186.0 37.1 %collective-permute-start.19 = (bf16[256,2048]{1,0:T(8,128)(2,1)}, bf16[256,2048]{1,0:T(8,128)(2,1)}, u32[]{:S(2)}, u32[]{:S(2)}) collective-permute-start(bf16[256,2048]{1,0:T(8,128)(2,1)} %get-tuple-element.90), channel_id=1, source_target_pairs={{0,4},{12,8},{1,5},{13,9},{2,6},{14,10},{3,7},{15,11},{16,20},{28,... | collective-permute-start | bytes 3145736 | tf_op jit(solution)/shard_map/ppermute | solution.py:99
  187.3 24.0 %collective-permute-start.20 = (bf16[192,2048]{1,0:T(8,128)(2,1)}, bf16[192,2048]{1,0:T(8,128)(2,1)}, u32[]{:S(2)}, u32[]{:S(2)}) collective-permute-start(bf16[192,2048]{1,0:T(8,128)(2,1)} %collective-permute-done.18.refs_4_.refs_3_), channel_id=1, source_target_pairs={{4,0},{8,12},{5,1},{9,13},{6,2},{10,14},{7,3},{11,15},{20,16},{24,... | collective-permute-start | bytes 2359304 | tf_op jit(solution)/shard_map/ppermute | solution.py:75
  225.3 17.0 %collective-permute-start.21 = (bf16[256,2048]{1,0:T(8,128)(2,1)}, bf16[256,2048]{1,0:T(8,128)(2,1)}, u32[]{:S(2)}, u32[]{:S(2)}) collective-permute-start(bf16[256,2048]{1,0:T(8,128)(2,1)} %get-tuple-element.96), channel_id=1, source_target_pairs={{0,4},{12,8},{1,5},{13,9},{2,6},{14,10},{3,7},{15,11},{16,20},{28,... | collective-permute-start | bytes 3145736 | tf_op jit(solution)/shard_map/ppermute | solution.py:104
  227.1 17.2 %collective-permute-start.22 = (bf16[256,2048]{1,0:T(8,128)(2,1)S(1)}, bf16[256,2048]{1,0:T(8,128)(2,1)S(1)}, u32[]{:S(2)}, u32[]{:S(2)}) collective-permute-start(bf16[256,2048]{1,0:T(8,128)(2,1)S(1)} %add_convert_fusion.3), channel_id=1, source_target_pairs={{4,8},{8,4},{5,9},{9,5},{6,10},{10,6},{7,11},{11,7},{20,24},{24,20... | collective-permute-start | bytes 3145736 | tf_op jit(solution)/shard_map/ppermute | solution.py:105
  259.6 39.5 %collective-permute-start.25 = (bf16[128,2048]{1,0:T(8,128)(2,1)}, bf16[128,2048]{1,0:T(8,128)(2,1)}, u32[]{:S(2)}, u32[]{:S(2)}) collective-permute-start(bf16[128,2048]{1,0:T(8,128)(2,1)} %get-tuple-element.105), channel_id=1, source_target_pairs={{0,4},{12,8},{1,5},{13,9},{2,6},{14,10},{3,7},{15,11},{16,20},{28,... | collective-permute-start | bytes 1572872 | tf_op jit(solution)/shard_map/ppermute | solution.py:99
  262.7 44.0 %all-to-all-start = ((bf16[4,2,128,512]{3,2,1,0:T(8,128)(2,1)}), bf16[4,2,128,512]{3,2,1,0:T(8,128)(2,1)}, u32[]{:S(2)}, u32[]{:S(2)}) async-start(bf16[4,2,128,512]{3,2,1,0:T(8,128)(2,1)} %copy.35), calls=%async_computation | async-start | bytes 2097152 | tf_op jit(solution)/shard_map/all_to_all | solution.py:755
  294.0 34.0 %collective-permute-start.23 = (bf16[256,2048]{1,0:T(8,128)(2,1)S(1)}, bf16[256,2048]{1,0:T(8,128)(2,1)}, u32[]{:S(2)}, u32[]{:S(2)}) collective-permute-start(bf16[256,2048]{1,0:T(8,128)(2,1)S(1)} %add_convert_fusion.2.refs_3_), channel_id=1, source_target_pairs={{4,8},{8,4},{5,9},{9,5},{6,10},{10,6},{7,11},{11,7},{20,24},{24,20... | collective-permute-start | bytes 3145736 | tf_op jit(solution)/shard_map/ppermute | solution.py:119
  297.5 31.3 %collective-permute-start.24 = (bf16[256,2048]{1,0:T(8,128)(2,1)S(1)}, bf16[256,2048]{1,0:T(8,128)(2,1)}, u32[]{:S(2)}, u32[]{:S(2)}) collective-permute-start(bf16[256,2048]{1,0:T(8,128)(2,1)S(1)} %add_convert_fusion.1.refs_4_), channel_id=1, source_target_pairs={{0,4},{4,0},{8,12},{12,8},{1,5},{5,1},{9,13},{13,9},{2,6},{6,2},{1... | collective-permute-start | bytes 3145736 | tf_op jit(solution)/shard_map/ppermute | solution.py:120
  306.7 40.4 %collective-permute-start.26 = (bf16[128,2048]{1,0:T(8,128)(2,1)}, bf16[128,2048]{1,0:T(8,128)(2,1)}, u32[]{:S(2)}, u32[]{:S(2)}) collective-permute-start(bf16[128,2048]{1,0:T(8,128)(2,1)} %copy-done.33), channel_id=1, source_target_pairs={{0,4},{12,8},{1,5},{13,9},{2,6},{14,10},{3,7},{15,11},{16,20},{28,... | collective-permute-start | bytes 1572872 | tf_op jit(solution)/shard_map/ppermute | solution.py:104
  309.9 38.4 %collective-permute-start.27 = (bf16[128,2048]{1,0:T(8,128)(2,1)}, bf16[128,2048]{1,0:T(8,128)(2,1)}, u32[]{:S(2)}, u32[]{:S(2)}) collective-permute-start(bf16[128,2048]{1,0:T(8,128)(2,1)} %add_convert_fusion.7.refs_6_), channel_id=1, source_target_pairs={{4,8},{8,4},{5,9},{9,5},{6,10},{10,6},{7,11},{11,7},{20,24},{24,20... | collective-permute-start | bytes 1572872 | tf_op jit(solution)/shard_map/ppermute | solution.py:105
  342.4 23.6 %collective-permute-start.31 = (bf16[64,2048]{1,0:T(8,128)(2,1)S(1)}, bf16[64,2048]{1,0:T(8,128)(2,1)S(1)}, u32[]{:S(2)}, u32[]{:S(2)}) collective-permute-start(bf16[64,2048]{1,0:T(8,128)(2,1)S(1)} %get-tuple-element.114), channel_id=1, source_target_pairs={{0,8},{4,12},{8,0},{12,4},{1,9},{5,13},{9,1},{13,5},{2,10},{6,14},... | collective-permute-start | bytes 786440 | tf_op jit(solution)/shard_map/ppermute | solution.py:792
  346.5 23.1 %collective-permute-start.32 = (bf16[64,2048]{1,0:T(8,128)(2,1)S(1)}, bf16[64,2048]{1,0:T(8,128)(2,1)S(1)}, u32[]{:S(2)}, u32[]{:S(2)}) collective-permute-start(bf16[64,2048]{1,0:T(8,128)(2,1)S(1)} %get-tuple-element.115), channel_id=1, source_target_pairs={{0,12},{4,0},{8,4},{12,8},{1,13},{5,1},{9,5},{13,9},{2,14},{6,2},{... | collective-permute-start | bytes 786440 | tf_op jit(solution)/shard_map/ppermute | solution.py:792
  349.6 30.4 %collective-permute-start.28 = (bf16[128,2048]{1,0:T(8,128)(2,1)S(1)}, bf16[128,2048]{1,0:T(8,128)(2,1)S(1)}, u32[]{:S(2)}, u32[]{:S(2)}) collective-permute-start(bf16[128,2048]{1,0:T(8,128)(2,1)S(1)} %add_convert_fusion.6), channel_id=1, source_target_pairs={{4,8},{8,4},{5,9},{9,5},{6,10},{10,6},{7,11},{11,7},{20,24},{24,20... | collective-permute-start | bytes 1572872 | tf_op jit(solution)/shard_map/ppermute | solution.py:119
  353.0 27.0 %collective-permute-start.29 = (bf16[128,2048]{1,0:T(8,128)(2,1)S(1)}, bf16[128,2048]{1,0:T(8,128)(2,1)S(1)}, u32[]{:S(2)}, u32[]{:S(2)}) collective-permute-start(bf16[128,2048]{1,0:T(8,128)(2,1)S(1)} %add_convert_fusion.5), channel_id=1, source_target_pairs={{0,4},{4,0},{8,12},{12,8},{1,5},{5,1},{9,13},{13,9},{2,6},{6,2},{1... | collective-permute-start | bytes 1572872 | tf_op jit(solution)/shard_map/ppermute | solution.py:120
  (58 other events, 744.6 us)
